TPU v7x, 32 devices: a whole 2x2x4 slice. The times are simulated.
32 devices in a mesh: groups: 2 (over y), tensor: 16 (over z, x, core).
Axes of the slice: x: 2, y: 2, z: 4, core: 2. Of those that a mesh axis runs over, the one named last changes fastest.
Arguments:
- tokens: bfloat16 [2048, 8192], P(('groups', 'tensor')), parts along dimension 0, may hold values from -6 to 6
- gate_matrix: bfloat16 [8192, 28672], P(None, 'tensor'), may hold values from -0.0625 to 0.0625
- up_matrix: bfloat16 [8192, 28672], P(None, 'tensor'), may hold values from -0.0625 to 0.0625
- lowrank_down: bfloat16 [16, 64, 8192], P('tensor'), may hold values from -0.0625 to 0.0625
- lowrank_up: bfloat16 [16, 64, 28672], P(None, None, 'tensor'), may hold values from -0.75 to 0.75
- tenant: int32 [16], P('groups'), parts along dimension 0, may hold values from 0 to 15, as said below
- adapter_storage_slot: int32 [16], replicated, may hold values from 0 to 15, each once
- live_count: int32 [16], P('groups'), parts along dimension 0, may hold values from 1 to 128
Outputs:
- hidden: bfloat16 [2048, 28672], P('groups', 'tensor'), parts along dimension 0
There are 2 independent parts, one for each index of `groups`. A program takes and returns all parts, laid end to end along the dimension named above; an argument that names none is the same for every part. Nothing has to cross between parts.
Inputs may be any that keep to these rules, and one draw needn't show every extreme that they name: `tenant`: not all blocks name the same adapter. `adapter_storage_slot`: each storage slot holds exactly one adapter.
All inputs are finite; a program needn't handle non-finite values.
Results may differ from a plain program's by a relative error of at most 0.0046.
Values may be sent and summed in bfloat16 or wider, within the bound.
No kernel may reach another device: no remote copies, remote signals or barrier semaphores. Data moves between devices by JAX's collectives and lax.ppermute only.
A program may use at most 192 MiB of HBM per device.

v0:
```python
import jax
import jax.numpy as jnp
from jax import lax
from jax.sharding import PartitionSpec as P

lowrank_scale = 2.0


def on_device(
    tokens,
    gate_matrix,
    up_matrix,
    lowrank_down,
    lowrank_up,
    tenant,
    adapter_storage_slot,
    live_count,
):
    my_index = lax.axis_index("tensor")
    gathered = lax.all_gather(tokens, "tensor", axis=0, tiled=True)
    row_total = gathered.shape[0]
    width = gathered.shape[1]
    block_count = tenant.shape[0]
    block_len = row_total // block_count
    hidden_columns = gate_matrix.shape[1]
    gate_out = jnp.dot(gathered, gate_matrix, preferred_element_type=jnp.float32)
    up_output = jnp.dot(gathered, up_matrix, preferred_element_type=jnp.float32)
    slot_numbers = adapter_storage_slot[tenant]
    rows_block = gathered.reshape(block_count, block_len, width)
    per_replica = lowrank_down.shape[0]
    rank_width = lowrank_down.shape[1]
    first_slot = my_index * per_replica
    pieces = []
    for block in range(block_count):
        slot_here = slot_numbers[block]
        mine = jnp.logical_and(slot_here >= first_slot, slot_here < first_slot + per_replica)
        resident_slot = jnp.clip(slot_here - first_slot, 0, per_replica - 1)
        down_matrix = lax.dynamic_index_in_dim(lowrank_down, resident_slot, 0, keepdims=False)
        block_rows = rows_block[block]

        def product_fn(rows_in=block_rows, map_in=down_matrix):
            return lax.dot_general(
                rows_in, map_in, (((1,), (1,)), ((), ())), preferred_element_type=jnp.float32
            )

        def empty_fn():
            return jnp.zeros((block_len, rank_width), jnp.float32)

        pieces.append(lax.cond(mine, product_fn, empty_fn))
    partial_value = jnp.stack(pieces, axis=0)
    reduced_output = lax.psum(partial_value, "tensor").astype(jnp.bfloat16)
    every_slot = jnp.arange(lowrank_up.shape[0], dtype=jnp.int32)
    slot_indicator = (slot_numbers[:, None] == every_slot[None, :]).astype(jnp.bfloat16)
    adapter_up = jnp.einsum(
        "oe,exz->oxz", slot_indicator, lowrank_up, preferred_element_type=jnp.float32
    ).astype(jnp.bfloat16)
    lowrank_term = jnp.einsum(
        "who,wok->whk", reduced_output, adapter_up, preferred_element_type=jnp.float32
    )
    up_output = up_output + lowrank_scale * lowrank_term.reshape(row_total, hidden_columns)
    positions = jnp.arange(block_len, dtype=jnp.int32)
    live_rows = (positions[None, :] < live_count[:, None]).reshape(row_total, 1)
    hidden = jnp.where(live_rows, jax.nn.silu(gate_out) * up_output, 0.0)
    return hidden.astype(jnp.bfloat16)


def solution(mesh):
    placed = (
        P(("groups", "tensor"), None),
        P(None, "tensor"),
        P(None, "tensor"),
        P("tensor", None, None),
        P(None, None, "tensor"),
        P("groups"),
        P(),
        P("groups"),
    )
    return jax.shard_map(
        on_device, mesh=mesh, in_specs=placed, out_specs=P("groups", "tensor"), check_vma=False
    )
```

profile of v0, /device:TPU:4, one launch (start us, length us, event | category | flops | bytes accessed | tf_op | source)
XLA Modules:
  0.0 287.3 jit_solution(9920644691950973308)
XLA Ops:
  6.5 0.0 copy-start
  6.5 0.0 all-gather.2.cloned.1.call-start
  6.5 0.7 all-gather.2.cloned.1.call-update
  7.3 0.7 compare_select_fusion
  7.9 0.0 copy-done
  7.9 0.6 gather_fusion
  8.6 0.7 fusion.50
  19.3 0.7 fusion.46
  20.0 5.3 %fusion.43 = bf16[8,64,1792]{2,0,1:T(8,128)(2,1)S(1)} fusion(bf16[16,64,1792]{2,1,0:T(8,128)(2,1)} %param.28, s32[8]{0:T(128)S(1)} %gather_fusion), kind=kOutput, calls=%fused_computation.31 | convolution fusion | flops 29360256 | bytes 5505056 | tf_op jit(solution)/shard_map/oe,exz->oxz/dot_general | solution.py:54
  25.3 112.4 %all-gather.2.cloned.1.call-done = bf16[1024,8192]{1,0:T(8,128)(2,1)} async-done(((bf16[64,8192]{1,0:T(8,128)(2,1)}), bf16[1024,8192]{1,0:T(8,128)(2,1)}) %all-gather.2.cloned.1.call-update) | async-done | bytes 16777232 | tf_op jit(solution)/shard_map/all_gather | solution.py:20
  137.7 2.7 conditional.13
  137.7 2.7 fusion.27
  140.7 62.0 %all-reduce.1 = bf16[8,128,64]{1,2,0:T(8,128)(2,1)S(1)} all-reduce(f32[8,128,64]{1,2,0:T(8,128)S(1)} %constant_dynamic-update-slice_fusion), channel_id=1, replica_groups=mesh['groups'=2,'tensor'=16] {'tensor'}, use_global_device_ids=true, to_apply=%region_16.17 | all-reduce | flops 65536 | bytes 393216 | tf_op jit(solution)/shard_map/psum | solution.py:51
  202.7 1.2 convolution_multiply_fusion
  203.9 35.8 %fusion.51 = f32[1024,1792]{1,0:T(8,128)S(1)} fusion(bf16[1024,8192]{1,0:T(8,128)(2,1)} %all-gather.2.cloned.1.call-done, bf16[8192,1792]{1,0:T(8,128)(2,1)} %param.25), kind=kOutput, calls=%fused_computation.50 | convolution fusion | flops 30064771072 | bytes 53477376 | tf_op jit(solution)/shard_map/dot_general | solution.py:26
  239.7 0.0 copy-start.1
  239.7 40.7 %fusion.42 = bf16[1024,1792]{1,0:T(8,128)(2,1)} fusion(f32[8,128,1792]{2,1,0:T(8,128)S(1)} %convolution_multiply_fusion, f32[1024,1792]{1,0:T(8,128)S(1)} %fusion.51, bf16[1024,8192]{1,0:T(8,128)(2,1)} %all-gather.2.cloned.1.call-done, bf16[8192,1792]{1,0:T(8,128)(2,1)} %param.26, pred[1024]{0:T(1024)(128)(4,1)S(1)} %fusion.46), kind=kOutput, calls=%fused_computation.28 | convolution fusion | flops 30079451136 | bytes 64488448 | tf_op jit(solution)/shard_map/dot_general | solution.py:27
  280.4 0.0 copy-done.1
  (23 shorter events, 0.2 us)
Async XLA Ops:
  6.5 1.4 copy-start
  6.5 131.1 %all-gather.2.cloned.1.call-start = ((), (), s32[]{:S(2)}) async-start(), calls=%async_computation | async-start | bytes 17825792 | tf_op jit(solution)/shard_map/all_gather | solution.py:20
  239.7 40.7 %copy-start.1 = (s32[16]{0:T(128)S(1)}, s32[16]{0:T(128)}, u32[]{:S(2)}) copy-start(s32[16]{0:T(128)} %param.30) | copy-start | bytes 196
Sparse Core Ops, SparseCore 0:
  9.5 128.0 all-gather.1
where the time goes:
time: 291 us; the launch traced here: 287 us
  waiting for transfers between devices  113 us (39%)
  matrix products  85.7 us (29%)
  blocking collectives  62 us (21%)
  between operations  23.5 us (8%)
    all_gather x1, waiting for transfers between devices, on_device(): gathered = lax.all_gather(tokens, 'tensor', axis=0, tiled=True)  112 us
    psum x1, blocking collectives, on_device(): reduced_output = lax.psum(partial_value, 'tensor').astype(jnp.bfloat16)  62 us
    dot_general x1, matrix products, on_device(): up_output = jnp.dot(gathered, up_matrix, preferred_element_type=jnp.float32)  40.7 us
    dot_general x1, matrix products, on_device(): jnp.dot(gathered, gate_matrix, preferred_element_type=jnp.float32)  35.8 us
  transfers between devices with their start and end apart: 1, of which 1 were waited for; matrix products, arithmetic and copies ran while one was open for 3% of the time, Pallas kernels for 0%

commit v1 on v0

--- a/solution.py
+++ b/solution.py
@@ -1,9 +1,297 @@
 import jax
 import jax.numpy as jnp
 from jax import lax
+from jax.experimental import pallas as pl
+from jax.experimental.pallas import tpu as pltpu
 from jax.sharding import PartitionSpec as P
 
 lowrank_scale = 2.0
+TILE = 256
+VMEM_LIMIT = 48 * 1024 * 1024
+
+
+def chip_at(place, chips):
+    half = chips // 2
+    if place < half:
+        return 2 * place
+    return 2 * (chips - 1 - place) + 1
+
+
+def ring_pairs(chips, step):
+    pairs = []
+    for place in range(chips):
+        for core in range(2):
+            pairs.append((2 * chip_at(place, chips) + core, 2 * chip_at((place + step) % chips, chips) + core))
+    return pairs
+
+
+def pass_call(meta, blocks, down, gate_matrix, up_matrix, earlier, first_tile, tiles, block_len, want_reduced):
+    width, columns = gate_matrix.shape
+    rank = down.shape[0]
+    row_total = earlier[0].shape[0] if not isinstance(earlier[0], tuple) else earlier[0][0]
+    fresh = isinstance(earlier[0], tuple)
+    count = len(blocks)
+    rows = count * block_len
+    half = block_len // 2
+    flat = []
+    places = []
+    for number, pieces in enumerate(blocks):
+        for piece, sibling, offset in pieces:
+            places.append((number * block_len, sibling, offset, piece.shape[0]))
+            flat.append(piece)
+    n_pieces = len(flat)
+
+    def kernel(*refs):
+        meta_ref = refs[0]
+        piece_refs = refs[1:1 + n_pieces]
+        rest = refs[1 + n_pieces:]
+        down_ref, gate_ref, up_ref = rest[:3]
+        rest = rest[3:]
+        if not fresh:
+            rest = rest[2:]
+        prod_ref, act_ref = rest[:2]
+        rest = rest[2:]
+        if want_reduced:
+            reduced_ref = rest[0]
+            rest = rest[1:]
+        held, prod_tile, act_tile, in_sem, out_sem = rest
+        step = pl.program_id(0)
+        slot = lax.rem(step, 2)
+
+        @pl.when(step == 0)
+        def _():
+            copies = []
+            for k in range(n_pieces):
+                base, sibling, offset, length = places[k]
+                core = meta_ref[0]
+                side = (1 - core) if sibling else core
+                start = pl.multiple_of(base + side * half + offset, 32)
+                copies.append(pltpu.make_async_copy(piece_refs[k], held.at[pl.ds(start, length)], in_sem.at[k]))
+            for copy in copies:
+                copy.start()
+            for copy in copies:
+                copy.wait()
+            if want_reduced:
+                found = lax.dot_general(held[...], down_ref[...], (((1,), (1,)), ((), ())), preferred_element_type=jnp.float32)
+                for b in range(count):
+                    part = found[b * block_len:(b + 1) * block_len]
+                    reduced_ref[b * block_len:(b + 1) * block_len, :] = jnp.where(meta_ref[1 + 3 * b + 2] == 1, part, 0.0).astype(jnp.bfloat16)
+
+        def out_copies(at_step, at_slot):
+            made = []
+            for b in range(count):
+                block_row = pl.multiple_of(meta_ref[1 + 3 * b] * block_len, block_len)
+                col = pl.multiple_of((at_step + first_tile) * TILE, TILE)
+                for n, (tile, out) in enumerate(((prod_tile, prod_ref), (act_tile, act_ref))):
+                    made.append(pltpu.make_async_copy(
+                        tile.at[at_slot, pl.ds(b * block_len, block_len)],
+                        out.at[pl.ds(block_row, block_len), pl.ds(col, TILE)],
+                        out_sem.at[at_slot, 2 * b + n]))
+            return made
+
+        @pl.when(step >= 2)
+        def _():
+            for copy in out_copies(step - 2, slot):
+                copy.wait()
+
+        rows_in = held[...]
+        gate_out = jnp.dot(rows_in, gate_ref[...], preferred_element_type=jnp.float32)
+        up_out = jnp.dot(rows_in, up_ref[...], preferred_element_type=jnp.float32)
+        for b in range(count):
+            at = slice(b * block_len, (b + 1) * block_len)
+            gate_part = gate_out[at]
+            act = gate_part / (1.0 + jnp.exp(-gate_part))
+            live = lax.broadcasted_iota(jnp.int32, act.shape, 0) < meta_ref[1 + 3 * b + 1]
+            act = jnp.where(live, act, 0.0)
+            prod = jnp.where(live, act * up_out[at], 0.0)
+            act_tile[slot, at, :] = act.astype(jnp.bfloat16)
+            prod_tile[slot, at, :] = prod.astype(jnp.bfloat16)
+        for copy in out_copies(step, slot):
+            copy.start()
+
+        @pl.when(step == tiles - 1)
+        def _():
+            if tiles > 1:
+                for copy in out_copies(step - 1, 1 - slot):
+                    copy.wait()
+            for copy in out_copies(step, slot):
+                copy.wait()
+
+    weight_spec = pl.BlockSpec((width, TILE), lambda j, m: (0, first_tile + j))
+    any_spec = pl.BlockSpec(memory_space=pl.ANY)
+    in_specs = [any_spec] * n_pieces + [pl.BlockSpec((rank, width), lambda j, m: (0, 0)), weight_spec, weight_spec]
+    operands = [meta] + flat + [down, gate_matrix, up_matrix]
+    aliases = {}
+    if not fresh:
+        in_specs += [any_spec, any_spec]
+        aliases = {len(operands): 0, len(operands) + 1: 1}
+        operands += list(earlier)
+    out_specs = [any_spec, any_spec]
+    out_shape = [jax.ShapeDtypeStruct((row_total, columns), jnp.bfloat16)] * 2
+    if want_reduced:
+        out_specs.append(pl.BlockSpec((rows, rank), lambda j, m: (0, 0)))
+        out_shape.append(jax.ShapeDtypeStruct((rows, rank), jnp.bfloat16))
+    return pl.pallas_call(
+        kernel,
+        grid_spec=pltpu.PrefetchScalarGridSpec(
+            num_scalar_prefetch=1,
+            grid=(tiles,),
+            in_specs=in_specs,
+            out_specs=out_specs,
+            scratch_shapes=[
+                pltpu.VMEM((rows, width), jnp.bfloat16),
+                pltpu.VMEM((2, rows, TILE), jnp.bfloat16),
+                pltpu.VMEM((2, rows, TILE), jnp.bfloat16),
+                pltpu.SemaphoreType.DMA((n_pieces,)),
+                pltpu.SemaphoreType.DMA((2, 2 * count)),
+            ],
+        ),
+        out_shape=out_shape,
+        input_output_aliases=aliases,
+        compiler_params=pltpu.CompilerParams(dimension_semantics=("arbitrary",), vmem_limit_bytes=VMEM_LIMIT),
+        cost_estimate=pl.CostEstimate(
+            flops=4 * rows * width * TILE * tiles, bytes_accessed=4 * width * TILE * tiles, transcendentals=0),
+    )(*operands)
+
+
+def table_call(meta, pieces, down, owned, row_total, block_len):
+    rank, width = down.shape
+    half = block_len // 2
+    n_pieces = len(pieces)
+    n_owned = len(owned)
+
+    def kernel(*refs):
+        meta_ref = refs[0]
+        piece_refs = refs[1:1 + n_pieces]
+        down_ref = refs[1 + n_pieces]
+        owned_refs = refs[2 + n_pieces:2 + n_pieces + n_owned]
+        table_ref, held, in_sem = refs[2 + n_pieces + n_owned:]
+        copies = []
+        for k, (piece, sibling, offset) in enumerate(pieces):
+            core = meta_ref[0]
+            side = (1 - core) if sibling else core
+            start = pl.multiple_of(side * half + offset, 32)
+            copies.append(pltpu.make_async_copy(piece_refs[k], held.at[pl.ds(start, piece.shape[0])], in_sem.at[k]))
+        for copy in copies:
+            copy.start()
+        number = 0
+        for ref in owned_refs:
+            for b in range(ref.shape[0] // block_len):
+                row = pl.multiple_of(meta_ref[1 + 3 * number] * block_len, block_len)
+                table_ref[pl.ds(row, block_len), :] = ref[b * block_len:(b + 1) * block_len, :]
+                number += 1
+        for copy in copies:
+            copy.wait()
+        found = lax.dot_general(held[...], down_ref[...], (((1,), (1,)), ((), ())), preferred_element_type=jnp.float32)
+        row = pl.multiple_of(meta_ref[1 + 3 * number] * block_len, block_len)
+        table_ref[pl.ds(row, block_len), :] = jnp.where(meta_ref[1 + 3 * number + 2] == 1, found, 0.0).astype(jnp.bfloat16)
+
+    whole = pl.BlockSpec(memory_space=pltpu.VMEM)
+    return pl.pallas_call(
+        kernel,
+        in_specs=[pl.BlockSpec(memory_space=pltpu.SMEM)] + [pl.BlockSpec(memory_space=pl.ANY)] * n_pieces + [whole] * (1 + n_owned),
+        out_specs=whole,
+        out_shape=jax.ShapeDtypeStruct((row_total, rank), jnp.bfloat16),
+        scratch_shapes=[pltpu.VMEM((block_len, width), jnp.bfloat16), pltpu.SemaphoreType.DMA((n_pieces,))],
+        compiler_params=pltpu.CompilerParams(vmem_limit_bytes=VMEM_LIMIT),
+        cost_estimate=pl.CostEstimate(flops=2 * block_len * width * 256, bytes_accessed=4 * 1024 * 1024, transcendentals=0),
+    )(meta, *[piece for piece, _, _ in pieces], down, *owned)
+
+
+def finish_call(slots, table, lowrank_up, prod, act, block_len):
+    row_total, columns = prod.shape
+    rank = table.shape[1]
+
+    def kernel(slots_ref, table_ref, map_ref, prod_ref, act_ref, out_ref):
+        term = jnp.dot(table_ref[...], map_ref[0], preferred_element_type=jnp.float32)
+        total = prod_ref[...].astype(jnp.float32) + act_ref[...].astype(jnp.float32) * (lowrank_scale * term)
+        out_ref[...] = total.astype(jnp.bfloat16)
+
+    row_spec = pl.BlockSpec((block_len, columns), lambda b, s: (b, 0))
+    return pl.pallas_call(
+        kernel,
+        grid_spec=pltpu.PrefetchScalarGridSpec(
+            num_scalar_prefetch=1,
+            grid=(row_total // block_len,),
+            in_specs=[
+                pl.BlockSpec((block_len, rank), lambda b, s: (b, 0)),
+                pl.BlockSpec((1, rank, columns), lambda b, s: (s[b], 0, 0)),
+                row_spec,
+                row_spec,
+            ],
+            out_specs=row_spec,
+        ),
+        out_shape=jax.ShapeDtypeStruct((row_total, columns), jnp.bfloat16),
+        input_output_aliases={3: 0},
+        compiler_params=pltpu.CompilerParams(dimension_semantics=("arbitrary",), vmem_limit_bytes=VMEM_LIMIT),
+        cost_estimate=pl.CostEstimate(
+            flops=2 * row_total * columns * 256, bytes_accessed=6 * row_total * columns, transcendentals=0),
+    )(slots, table, lowrank_up, prod, act)
+
+
+def on_ring(tokens, gate_matrix, up_matrix, lowrank_down, lowrank_up, tenant, adapter_storage_slot, live_count):
+    block_count = tenant.shape[0]
+    rows_here, width = tokens.shape
+    chips = block_count
+    block_len = 2 * rows_here
+    row_total = block_count * block_len
+    columns = gate_matrix.shape[1]
+    me = lax.axis_index("tensor")
+    core = lax.rem(me, 2)
+    chip = me // 2
+    place = jnp.where(lax.rem(chip, 2) == 0, chip // 2, chips - 1 - chip // 2)
+    order = jnp.array([0, -1, 1, -2, 2, -3, 3, -4], jnp.int32)
+    at = lax.rem(place + order + chips, chips)
+    numbers = jnp.where(at < chips // 2, 2 * at, 2 * (chips - 1 - at) + 1)
+    slots = adapter_storage_slot[tenant]
+    here = (slots == me).astype(jnp.int32)
+    fields = jnp.stack([numbers, live_count[numbers], here[numbers]], axis=1).astype(jnp.int32)
+
+    def meta_of(first, count):
+        return jnp.concatenate([core[None].astype(jnp.int32), fields[first:first + count].reshape(-1)])
+
+    right, left = ring_pairs(chips, 1), ring_pairs(chips, -1)
+    swap = [(d, d ^ 1) for d in range(2 * chips)]
+
+    def send(value, pairs):
+        return lax.ppermute(value, "tensor", pairs)
+
+    down = lowrank_down[0]
+    rest = (gate_matrix, up_matrix)
+    n_tiles = columns // TILE
+    from_left, from_right = tokens, tokens
+    other = send(tokens, swap)
+    blocks = [[(tokens, False, 0), (other, True, 0)]]
+    state = ((row_total, columns), (row_total, columns))
+    owned = []
+    first = 0
+    for step in range(3):
+        from_left = send(from_left, right)
+        from_right = send(from_right, left)
+        prod, act, part = pass_call(meta_of(first, len(blocks)), blocks, down, *rest, state, 0, n_tiles, block_len, True)
+        state = (prod, act)
+        owned.append(part)
+        first += len(blocks)
+        blocks = [[(v, False, 0), (send(v, swap), True, 0)] for v in (from_left, from_right)]
+    cut = rows_here // 2
+    last_low = send(from_left[:cut], right)
+    last_high = send(from_right[cut:], left)
+    prod, act, part = pass_call(meta_of(first, 2), blocks, down, *rest, state, 0, n_tiles, block_len, True)
+    state = (prod, act)
+    owned.append(part)
+    first += 2
+    pieces = [
+        (last_low, False, 0), (send(last_low, swap), True, 0),
+        (last_high, False, cut), (send(last_high, swap), True, cut),
+    ]
+    table = table_call(meta_of(0, block_count), pieces, down, owned, row_total, block_len)
+    for bit in (1, 2, 4, 8):
+        table = table + send(table, [(d, d ^ bit) for d in range(2 * chips)])
+    start = 0
+    for count in (2, 2, 2, 1):
+        state = pass_call(meta_of(first, 1), [pieces], down, *rest, state, start, count, block_len, False)
+        start += count
+    return finish_call(slots, table, lowrank_up, *state, block_len)
 
 
 def on_device(
@@ -75,6 +363,7 @@
         P(),
         P("groups"),
     )
+    run = on_ring if mesh.shape["tensor"] == 16 else on_device
     return jax.shard_map(
-        on_device, mesh=mesh, in_specs=placed, out_specs=P("groups", "tensor"), check_vma=False
+        run, mesh=mesh, in_specs=placed, out_specs=P("groups", "tensor"), check_vma=False
     )

time: 291 us -> 197 us (0.68)
  Pallas kernels: 0 us -> 150 us
  waiting for transfers between devices: 113 us -> 20.7 us
  matrix products: 85.7 us -> 0 us
  blocking collectives: 62 us -> 0 us
  between operations: 23.5 us -> 0.26 us
  starting transfers between devices: 0.01 us -> 16 us
  local copies, waits for them, and re-layouts: 1.41 us -> 6.08 us
    pallas_call x0 -> x10, Pallas kernels: none -> 150 us  [the longest x8 140 us: pass_call(): pl.pallas_call(kernel, grid_spec=pltpu.PrefetchScalarGridSpec(num_scalar_...]
    all_gather x1 -> x0, waiting for transfers between devices: 112 us -> none  [on_device(): gathered = lax.all_gather(tokens, 'tensor', axis=0, tiled=True)]
    dot_general x5 -> x0, matrix products: 85.7 us -> none  [the longest x1 40.7 us: on_device(): up_output = jnp.dot(gathered, up_matrix, preferred_element_type=jnp.float32)]
    psum x1 -> x0, blocking collectives: 62 us -> none  [on_device(): reduced_output = lax.psum(partial_value, 'tensor').astype(jnp.bfloat16)]
    ppermute x0 -> x21, waiting for transfers between devices: none -> 20.7 us  [send(): return lax.ppermute(value, 'tensor', pairs)]
    ppermute x0 -> x21, starting transfers between devices: none -> 16 us  [send(): return lax.ppermute(value, 'tensor', pairs)]
  transfers between devices with their start and end apart: 1 -> 21, of which waited for: 1 -> 2; matrix products, arithmetic and copies ran while one was open for 3% -> 3% of each run, Pallas kernels for 0% -> 72%
where the time goes in v1:
time: 197 us; the launch traced here: 195 us
  Pallas kernels  150 us (76%)
  waiting for transfers between devices  20.7 us (11%)
  starting transfers between devices  16 us (8%)
  local copies, waits for them, and re-layouts  6.08 us (3%)
  other arithmetic  2.1 us (1%)
    pallas_call x8, Pallas kernels, pass_call(): pl.pallas_call(kernel, grid_spec=pltpu.PrefetchScalarGridSpec(num_scalar_...  140 us
    ppermute x21, waiting for transfers between devices, send(): return lax.ppermute(value, 'tensor', pairs)  20.7 us
    ppermute x21, starting transfers between devices, send(): return lax.ppermute(value, 'tensor', pairs)  16 us
    pallas_call x1, Pallas kernels, finish_call(): pl.pallas_call(kernel, grid_spec=pltpu.PrefetchScalarGridSpec(num_scalar_...  8.59 us
  transfers between devices with their start and end apart: 21, of which 2 were waited for; matrix products, arithmetic and copies ran while one was open for 3% of the time, Pallas kernels for 72%

profile of v1, /device:TPU:4, one launch (start us, length us, event | category | flops | bytes accessed | tf_op | source)
XLA Modules:
  0.0 194.7 jit_solution(7162781825532737712)
XLA Ops:
  0.0 1.6 collective-permute-start
  1.6 0.4 collective-permute-start.5
  2.1 0.7 compare_select_fusion.1
  2.8 0.6 gather_fusion
  3.4 0.7 compare_select_fusion
  4.1 1.3 gather_fusion.1
  5.4 0.6 gather_fusion.2
  6.1 0.1 copy.30
  6.2 0.1 reshape.23
  6.3 0.2 slice_reduce_fusion
  6.5 0.1 pad_add_fusion.2.refs_0_
  6.6 19.2 %collective-permute-done.refs_1_ = bf16[64,8192]{1,0:T(8,128)(2,1)S(1)} collective-permute-done((bf16[64,8192]{1,0:T(8,128)(2,1)}, bf16[64,8192]{1,0:T(8,128)(2,1)S(1)}, u32[]{:S(2)}, u32[]{:S(2)}) %collective-permute-start) | collective-permute-done | bytes 1048608 | tf_op jit(solution)/shard_map/ppermute | solution.py:257
  25.8 1.6 collective-permute-start.1
  27.4 0.2 collective-permute-start.12
  27.6 0.4 collective-permute-start.6
  28.1 0.1 pad_add_fusion.3.refs_0_
  28.1 0.1 copy.29
  28.2 0.1 copy.31
  28.3 0.1 reshape.24
  28.4 0.1 copy.32
  28.5 0.1 reshape.25
  28.6 0.1 reshape.21
  28.6 0.1 pad_add_fusion.4.refs_0_
  28.9 1.2 copy-done.2
  30.1 1.2 copy-done.5
  31.3 21.8 %shard_map.91 = (bf16[1024,1792]{1,0:T(8,128)(2,1)}, bf16[1024,1792]{1,0:T(8,128)(2,1)}, bf16[128,64]{1,0:T(8,128)(2,1)S(1)}) custom-call(s32[4]{0:T(128)S(1)} %pad_add_fusion.2.refs_0_, bf16[64,8192]{1,0:T(8,128)(2,1)S(1)} %copy-done.5, bf16[64,8192]{1,0:T(8,128)(2,1)S(1)} %collective-permute-done.10.refs_2_, bf16[64,8192]{1,0:T(8,128)(2,1)S(1)} %bitcast.5, ...), custom_call_target="tpu_custom_call" | custom-call | flops 7516192768 | bytes 58720256 | tf_op jit(solution)/shard_map/pallas_call | solution.py:134
  53.2 1.6 collective-permute-start.2
  54.8 0.2 collective-permute-start.14
  55.0 0.5 collective-permute-start.7
  55.4 29.6 %shard_map.92 = (bf16[1024,1792]{1,0:T(8,128)(2,1)}, bf16[1024,1792]{1,0:T(8,128)(2,1)}, bf16[256,64]{1,0:T(8,128)(2,1)S(1)}) custom-call(s32[7]{0:T(128)S(1)} %pad_add_fusion.3.refs_0_, bf16[64,8192]{1,0:T(8,128)(2,1)S(1)} %collective-permute-done.refs_1_, ...), custom_call_target="tpu_custom_call", output_to_operand_aliasing={{0}: (8, {}), {1}: (9, {})} | custom-call | flops 15032385536 | bytes 58720256 | tf_op jit(solution)/shard_map/pallas_call | solution.py:134
  85.1 1.6 collective-permute-start.3
  86.7 0.7 collective-permute-start.8
  87.4 0.5 collective-permute-start.16
  87.9 29.6 %shard_map.93 = (bf16[1024,1792]{1,0:T(8,128)(2,1)}, bf16[1024,1792]{1,0:T(8,128)(2,1)}, bf16[256,64]{1,0:T(8,128)(2,1)S(1)}) custom-call(s32[7]{0:T(128)S(1)} %pad_add_fusion.4.refs_0_, bf16[64,8192]{1,0:T(8,128)(2,1)} %collective-permute-done.1.refs_1_, ...), custom_call_target="tpu_custom_call", output_to_operand_aliasing={{0}: (8, {}), {1}: (9, {})} | custom-call | flops 15032385536 | bytes 58720256 | tf_op jit(solution)/shard_map/pallas_call | solution.py:134
  117.6 0.1 collective-permute-start.4
  117.6 0.5 collective-permute-start.9
  118.1 26.7 %shard_map.94 = (bf16[1024,1792]{1,0:T(8,128)(2,1)}, bf16[1024,1792]{1,0:T(8,128)(2,1)}, bf16[256,64]{1,0:T(8,128)(2,1)S(1)}) custom-call(s32[7]{0:T(128)S(1)} %pad_add_fusion.5.refs_0_, bf16[64,8192]{1,0:T(8,128)(2,1)S(1)} %collective-permute-done.2.refs_1_, ...), custom_call_target="tpu_custom_call", output_to_operand_aliasing={{0}: (8, {}), {1}: (9, {})} | custom-call | flops 15032385536 | bytes 58720256 | tf_op jit(solution)/shard_map/pallas_call | solution.py:134
  144.9 1.5 shard_map.95
  146.3 0.1 collective-permute-start.17
  146.6 1.4 collective-permute-done.17
  148.0 1.5 collective-permute-start.18
  149.6 8.6 %shard_map.96 = (bf16[1024,1792]{1,0:T(8,128)(2,1)}, bf16[1024,1792]{1,0:T(8,128)(2,1)}) custom-call(s32[4]{0:T(128)S(1)} %pad_add_fusion.6.refs_0_, bf16[32,8192]{1,0:T(8,128)(2,1)S(1)} %collective-permute-done.3.refs_1_, bf16[32,8192]{1,0:T(8,128)(2,1)S(1)} %collective-permute-done.4.refs_2_, ...), custom_call_target="tpu_custom_call", output_to_operand_aliasing={{0}: (8, {}), {1}: (9, {})} | custom-call | flops 2147483648 | bytes 16777216 | tf_op jit(solution)/shard_map/pallas_call | solution.py:134
  158.2 1.7 collective-permute-start.19
  159.9 8.5 %shard_map.97 = (bf16[1024,1792]{1,0:T(8,128)(2,1)}, bf16[1024,1792]{1,0:T(8,128)(2,1)}) custom-call(s32[4]{0:T(128)S(1)} %pad_add_fusion.6.refs_0_, bf16[32,8192]{1,0:T(8,128)(2,1)S(1)} %collective-permute-done.3.refs_1_, bf16[32,8192]{1,0:T(8,128)(2,1)S(1)} %collective-permute-done.4.refs_2_, ...), custom_call_target="tpu_custom_call", output_to_operand_aliasing={{0}: (8, {}), {1}: (9, {})} | custom-call | flops 2147483648 | bytes 16777216 | tf_op jit(solution)/shard_map/pallas_call | solution.py:134
  168.4 2.7 %collective-permute-start.20 = (bf16[1024,64]{1,0:T(8,128)(2,1)S(1)}, bf16[1024,64]{1,0:T(8,128)(2,1)S(1)}, u32[]{:S(2)}, u32[]{:S(2)}) collective-permute-start(bf16[1024,64]{1,0:T(8,128)(2,1)S(1)} %add.41), channel_id=1, source_target_pairs={{0,8},{1,9},{2,10},{3,11},{4,12},{5,13},{6,14},{7,15},{8,0},{9,1},... | collective-permute-start | bytes 393224 | tf_op jit(solution)/shard_map/ppermute | solution.py:257
  171.1 8.5 %shard_map.98 = (bf16[1024,1792]{1,0:T(8,128)(2,1)}, bf16[1024,1792]{1,0:T(8,128)(2,1)}) custom-call(s32[4]{0:T(128)S(1)} %pad_add_fusion.6.refs_0_, bf16[32,8192]{1,0:T(8,128)(2,1)S(1)} %collective-permute-done.3.refs_1_, bf16[32,8192]{1,0:T(8,128)(2,1)S(1)} %collective-permute-done.4.refs_2_, ...), custom_call_target="tpu_custom_call", output_to_operand_aliasing={{0}: (8, {}), {1}: (9, {})} | custom-call | flops 2147483648 | bytes 16777216 | tf_op jit(solution)/shard_map/pallas_call | solution.py:134
  179.6 6.5 %shard_map.99 = (bf16[1024,1792]{1,0:T(8,128)(2,1)}, bf16[1024,1792]{1,0:T(8,128)(2,1)}) custom-call(s32[4]{0:T(128)S(1)} %pad_add_fusion.6.refs_0_, bf16[32,8192]{1,0:T(8,128)(2,1)S(1)} %collective-permute-done.3.refs_1_, bf16[32,8192]{1,0:T(8,128)(2,1)S(1)} %collective-permute-done.4.refs_2_, ...), custom_call_target="tpu_custom_call", output_to_operand_aliasing={{0}: (8, {}), {1}: (9, {})} | custom-call | flops 1073741824 | bytes 8388608 | tf_op jit(solution)/shard_map/pallas_call | solution.py:134
  186.1 8.6 %shard_map.100 = bf16[1024,1792]{1,0:T(8,128)(2,1)} custom-call(s32[8]{0:T(128)S(1)} %gather_fusion, bf16[1024,64]{1,0:T(8,128)(2,1)S(1)} %add.42.table_ref, bf16[16,64,1792]{2,1,0:T(8,128)(2,1)S(1)} %copy-done.4, bf16[1024,1792]{1,0:T(8,128)(2,1)} %get-tuple-element.43.prod_ref, ...), custom_call_target="tpu_custom_call", output_to_operand_aliasing={{}: (3, {})} | custom-call | flops 939524096 | bytes 11010048 | tf_op jit(solution)/shard_map/pallas_call | solution.py:211
  (47 shorter events, 0.8 us)
Async XLA Ops:
  0.0 2.8 %copy-start = (s32[16]{0:T(128)S(1)}, s32[16]{0:T(128)}, u32[]{:S(2)}) copy-start(s32[16]{0:T(128)} %param.15) | copy-start | bytes 196
  0.0 28.9 %collective-permute-start.10 = (bf16[64,8192]{1,0:T(8,128)(2,1)}, bf16[64,8192]{1,0:T(8,128)(2,1)S(1)}, u32[]{:S(2)}, u32[]{:S(2)}) collective-permute-start(bf16[64,8192]{1,0:T(8,128)(2,1)} %refs_1_.1), channel_id=1, source_target_pairs={{0,1},{1,0},{2,3},{3,2},{4,5},{5,4},{6,7},{7,6},{8,9},{9,8},{10,11... | collective-permute-start | bytes 3145736 | tf_op jit(solution)/shard_map/ppermute | solution.py:257
  0.0 25.8 %collective-permute-start = (bf16[64,8192]{1,0:T(8,128)(2,1)}, bf16[64,8192]{1,0:T(8,128)(2,1)S(1)}, u32[]{:S(2)}, u32[]{:S(2)}) collective-permute-start(bf16[64,8192]{1,0:T(8,128)(2,1)} %refs_1_.1), channel_id=1, source_target_pairs={{0,4},{1,5},{4,8},{5,9},{8,12},{9,13},{12,14},{13,15},{14,10},{15,... | collective-permute-start | bytes 3145736 | tf_op jit(solution)/shard_map/ppermute | solution.py:257
  1.6 25.7 %collective-permute-start.5 = (bf16[64,8192]{1,0:T(8,128)(2,1)}, bf16[64,8192]{1,0:T(8,128)(2,1)S(1)}, u32[]{:S(2)}, u32[]{:S(2)}) collective-permute-start(bf16[64,8192]{1,0:T(8,128)(2,1)} %refs_1_.1), channel_id=1, source_target_pairs={{0,2},{1,3},{4,0},{5,1},{8,4},{9,5},{12,8},{13,9},{14,12},{15,13},... | collective-permute-start | bytes 3145736 | tf_op jit(solution)/shard_map/ppermute | solution.py:257
  25.8 29.2 %collective-permute-start.11 = (bf16[64,8192]{1,0:T(8,128)(2,1)S(1)}, bf16[64,8192]{1,0:T(8,128)(2,1)}, u32[]{:S(2)}, u32[]{:S(2)}) collective-permute-start(bf16[64,8192]{1,0:T(8,128)(2,1)S(1)} %collective-permute-done.refs_1_), channel_id=1, source_target_pairs={{0,1},{1,0},{2,3},{3,2},{4,5},{5,4},{6,7},{7,6},{8,9},{9,8},{10,11... | collective-permute-start | bytes 3145736 | tf_op jit(solution)/shard_map/ppermute | solution.py:257
  25.8 27.3 %collective-permute-start.1 = (bf16[64,8192]{1,0:T(8,128)(2,1)S(1)}, bf16[64,8192]{1,0:T(8,128)(2,1)}, u32[]{:S(2)}, u32[]{:S(2)}) collective-permute-start(bf16[64,8192]{1,0:T(8,128)(2,1)S(1)} %collective-permute-done.refs_1_), channel_id=1, source_target_pairs={{0,4},{1,5},{4,8},{5,9},{8,12},{9,13},{12,14},{13,15},{14,10},{15,... | collective-permute-start | bytes 3145736 | tf_op jit(solution)/shard_map/ppermute | solution.py:257
  27.4 28.1 %collective-permute-start.12 = (bf16[64,8192]{1,0:T(8,128)(2,1)S(1)}, bf16[64,8192]{1,0:T(8,128)(2,1)}, u32[]{:S(2)}, u32[]{:S(2)}) collective-permute-start(bf16[64,8192]{1,0:T(8,128)(2,1)S(1)} %collective-permute-done.5.refs_3_), channel_id=1, source_target_pairs={{0,1},{1,0},{2,3},{3,2},{4,5},{5,4},{6,7},{7,6},{8,9},{9,8},{10,11... | collective-permute-start | bytes 3145736 | tf_op jit(solution)/shard_map/ppermute | solution.py:257
  27.6 27.2 %collective-permute-start.6 = (bf16[64,8192]{1,0:T(8,128)(2,1)S(1)}, bf16[64,8192]{1,0:T(8,128)(2,1)}, u32[]{:S(2)}, u32[]{:S(2)}) collective-permute-start(bf16[64,8192]{1,0:T(8,128)(2,1)S(1)} %collective-permute-done.5.refs_3_), channel_id=1, source_target_pairs={{0,2},{1,3},{4,0},{5,1},{8,4},{9,5},{12,8},{13,9},{14,12},{15,13},... | collective-permute-start | bytes 3145736 | tf_op jit(solution)/shard_map/ppermute | solution.py:257
  28.9 1.2 copy-start.2
  30.1 1.2 copy-start.5
  31.3 24.1 %copy-start.3 = (bf16[1,64,8192]{2,1,0:T(8,128)(2,1)S(1)}, bf16[1,64,8192]{2,1,0:T(8,128)(2,1)}, u32[]{:S(2)}) copy-start(bf16[1,64,8192]{2,1,0:T(8,128)(2,1)} %param.12) | copy-start | bytes 3145732
  53.1 34.3 %collective-permute-start.13 = (bf16[64,8192]{1,0:T(8,128)(2,1)}, bf16[64,8192]{1,0:T(8,128)(2,1)S(1)}, u32[]{:S(2)}, u32[]{:S(2)}) collective-permute-start(bf16[64,8192]{1,0:T(8,128)(2,1)} %collective-permute-done.1.refs_1_), channel_id=1, source_target_pairs={{0,1},{1,0},{2,3},{3,2},{4,5},{5,4},{6,7},{7,6},{8,9},{9,8},{10,11... | collective-permute-start | bytes 3145736 | tf_op jit(solution)/shard_map/ppermute | solution.py:257
  53.2 31.8 %collective-permute-start.2 = (bf16[64,8192]{1,0:T(8,128)(2,1)}, bf16[64,8192]{1,0:T(8,128)(2,1)S(1)}, u32[]{:S(2)}, u32[]{:S(2)}) collective-permute-start(bf16[64,8192]{1,0:T(8,128)(2,1)} %collective-permute-done.1.refs_1_), channel_id=1, source_target_pairs={{0,4},{1,5},{4,8},{5,9},{8,12},{9,13},{12,14},{13,15},{14,10},{15,... | collective-permute-start | bytes 3145736 | tf_op jit(solution)/shard_map/ppermute | solution.py:257
  54.8 33.1 %collective-permute-start.14 = (bf16[64,8192]{1,0:T(8,128)(2,1)}, bf16[64,8192]{1,0:T(8,128)(2,1)S(1)}, u32[]{:S(2)}, u32[]{:S(2)}) collective-permute-start(bf16[64,8192]{1,0:T(8,128)(2,1)} %collective-permute-done.6.refs_3_), channel_id=1, source_target_pairs={{0,1},{1,0},{2,3},{3,2},{4,5},{5,4},{6,7},{7,6},{8,9},{9,8},{10,11... | collective-permute-start | bytes 3145736 | tf_op jit(solution)/shard_map/ppermute | solution.py:257
  55.0 31.7 %collective-permute-start.7 = (bf16[64,8192]{1,0:T(8,128)(2,1)}, bf16[64,8192]{1,0:T(8,128)(2,1)S(1)}, u32[]{:S(2)}, u32[]{:S(2)}) collective-permute-start(bf16[64,8192]{1,0:T(8,128)(2,1)} %collective-permute-done.6.refs_3_), channel_id=1, source_target_pairs={{0,2},{1,3},{4,0},{5,1},{8,4},{9,5},{12,8},{13,9},{14,12},{15,13},... | collective-permute-start | bytes 3145736 | tf_op jit(solution)/shard_map/ppermute | solution.py:257
  85.1 32.5 %collective-permute-start.3 = (bf16[32,8192]{1,0:T(8,128)(2,1)S(1)}, bf16[32,8192]{1,0:T(8,128)(2,1)S(1)}, u32[]{:S(2)}, u32[]{:S(2)}) collective-permute-start(bf16[32,8192]{1,0:T(8,128)(2,1)S(1)} %slice.37), channel_id=1, source_target_pairs={{0,4},{1,5},{4,8},{5,9},{8,12},{9,13},{12,14},{13,15},{14,10},{15,... | collective-permute-start | bytes 1572872 | tf_op jit(solution)/shard_map/ppermute | solution.py:257
  86.7 30.9 %collective-permute-start.8 = (bf16[32,8192]{1,0:T(8,128)(2,1)S(1)}, bf16[32,8192]{1,0:T(8,128)(2,1)S(1)}, u32[]{:S(2)}, u32[]{:S(2)}) collective-permute-start(bf16[32,8192]{1,0:T(8,128)(2,1)S(1)} %slice.38), channel_id=1, source_target_pairs={{0,2},{1,3},{4,0},{5,1},{8,4},{9,5},{12,8},{13,9},{14,12},{15,13},... | collective-permute-start | bytes 1572872 | tf_op jit(solution)/shard_map/ppermute | solution.py:257
  87.4 30.7 %collective-permute-start.15 = (bf16[64,8192]{1,0:T(8,128)(2,1)S(1)}, bf16[64,8192]{1,0:T(8,128)(2,1)S(1)}, u32[]{:S(2)}, u32[]{:S(2)}) collective-permute-start(bf16[64,8192]{1,0:T(8,128)(2,1)S(1)} %collective-permute-done.2.refs_1_), channel_id=1, source_target_pairs={{0,1},{1,0},{2,3},{3,2},{4,5},{5,4},{6,7},{7,6},{8,9},{9,8},{10,11... | collective-permute-start | bytes 3145736 | tf_op jit(solution)/shard_map/ppermute | solution.py:257
  87.4 30.7 %collective-permute-start.16 = (bf16[64,8192]{1,0:T(8,128)(2,1)S(1)}, bf16[64,8192]{1,0:T(8,128)(2,1)S(1)}, u32[]{:S(2)}, u32[]{:S(2)}) collective-permute-start(bf16[64,8192]{1,0:T(8,128)(2,1)S(1)} %collective-permute-done.7.refs_3_), channel_id=1, source_target_pairs={{0,1},{1,0},{2,3},{3,2},{4,5},{5,4},{6,7},{7,6},{8,9},{9,8},{10,11... | collective-permute-start | bytes 3145736 | tf_op jit(solution)/shard_map/ppermute | solution.py:257
  117.6 27.3 %collective-permute-start.4 = (bf16[32,8192]{1,0:T(8,128)(2,1)S(1)}, bf16[32,8192]{1,0:T(8,128)(2,1)S(1)}, u32[]{:S(2)}, u32[]{:S(2)}) collective-permute-start(bf16[32,8192]{1,0:T(8,128)(2,1)S(1)} %collective-permute-done.3.refs_1_), channel_id=1, source_target_pairs={{0,1},{1,0},{2,3},{3,2},{4,5},{5,4},{6,7},{7,6},{8,9},{9,8},{10,11... | collective-permute-start | bytes 1572872 | tf_op jit(solution)/shard_map/ppermute | solution.py:257
  117.6 27.2 %collective-permute-start.9 = (bf16[32,8192]{1,0:T(8,128)(2,1)S(1)}, bf16[32,8192]{1,0:T(8,128)(2,1)S(1)}, u32[]{:S(2)}, u32[]{:S(2)}) collective-permute-start(bf16[32,8192]{1,0:T(8,128)(2,1)S(1)} %collective-permute-done.8.refs_3_), channel_id=1, source_target_pairs={{0,1},{1,0},{2,3},{3,2},{4,5},{5,4},{6,7},{7,6},{8,9},{9,8},{10,11... | collective-permute-start | bytes 1572872 | tf_op jit(solution)/shard_map/ppermute | solution.py:257
  146.3 1.6 collective-permute-start.17
  148.0 10.1 %collective-permute-start.18 = (bf16[1024,64]{1,0:T(8,128)(2,1)S(1)}, bf16[1024,64]{1,0:T(8,128)(2,1)S(1)}, u32[]{:S(2)}, u32[]{:S(2)}) collective-permute-start(bf16[1024,64]{1,0:T(8,128)(2,1)S(1)} %add.39), channel_id=1, source_target_pairs={{0,2},{1,3},{2,0},{3,1},{4,6},{5,7},{6,4},{7,5},{8,10},{9,11},{10,... | collective-permute-start | bytes 393224 | tf_op jit(solution)/shard_map/ppermute | solution.py:257
  158.2 10.1 %collective-permute-start.19 = (bf16[1024,64]{1,0:T(8,128)(2,1)S(1)}, bf16[1024,64]{1,0:T(8,128)(2,1)S(1)}, u32[]{:S(2)}, u32[]{:S(2)}) collective-permute-start(bf16[1024,64]{1,0:T(8,128)(2,1)S(1)} %add.40), channel_id=1, source_target_pairs={{0,4},{1,5},{2,6},{3,7},{4,0},{5,1},{6,2},{7,3},{8,12},{9,13},{10,... | collective-permute-start | bytes 393224 | tf_op jit(solution)/shard_map/ppermute | solution.py:257
  168.4 17.6 %collective-permute-start.20 = (bf16[1024,64]{1,0:T(8,128)(2,1)S(1)}, bf16[1024,64]{1,0:T(8,128)(2,1)S(1)}, u32[]{:S(2)}, u32[]{:S(2)}) collective-permute-start(bf16[1024,64]{1,0:T(8,128)(2,1)S(1)} %add.41), channel_id=1, source_target_pairs={{0,8},{1,9},{2,10},{3,11},{4,12},{5,13},{6,14},{7,15},{8,0},{9,1},... | collective-permute-start | bytes 393224 | tf_op jit(solution)/shard_map/ppermute | solution.py:257
  179.5 6.6 %copy-start.4 = (bf16[16,64,1792]{2,1,0:T(8,128)(2,1)S(1)}, bf16[16,64,1792]{2,1,0:T(8,128)(2,1)}, u32[]{:S(2)}) copy-start(bf16[16,64,1792]{2,1,0:T(8,128)(2,1)} %map_ref.1) | copy-start | bytes 11010052
  186.1 8.6 %copy-start.1 = (s32[16]{0:T(128)S(1)}, s32[16]{0:T(128)}, u32[]{:S(2)}) copy-start(s32[16]{0:T(128)} %param.15) | copy-start | bytes 196

commit v2 on v1

v2 whole, which is shorter than its diff:
```python
import jax
import jax.numpy as jnp
from jax import lax
from jax.experimental import pallas as pl
from jax.experimental.pallas import tpu as pltpu
from jax.sharding import PartitionSpec as P

lowrank_scale = 2.0
TILE = 256
KEPT = 3
VMEM_LIMIT = 30 * 1024 * 1024


def chip_at(place, chips):
    half = chips // 2
    if place < half:
        return 2 * place
    return 2 * (chips - 1 - place) + 1


def ring_pairs(chips, step):
    pairs = []
    for place in range(chips):
        for core in range(2):
            pairs.append((2 * chip_at(place, chips) + core, 2 * chip_at((place + step) % chips, chips) + core))
    return pairs


def pass_call(meta, first, blocks, down, gate_matrix, up_matrix, kept, earlier, tiles, block_len, want_reduced):
    width, columns = gate_matrix.shape
    rank = down.shape[0]
    fresh = kept is None
    row_total = earlier[0] if fresh else earlier[0].shape[0]
    count = len(blocks)
    rows = count * block_len
    half = block_len // 2
    n_kept = len([t for t in tiles if t < KEPT])
    n_streamed = len(tiles) - n_kept
    first_streamed = KEPT
    flat = []
    places = []
    for number, pieces in enumerate(blocks):
        for piece, sibling, offset in pieces:
            places.append((number * block_len, sibling, offset, piece.shape[0]))
            flat.append(piece)
    n_pieces = len(flat)

    def kernel(*refs):
        meta_ref = refs[0]
        piece_refs = refs[1:1 + n_pieces]
        rest = refs[1 + n_pieces:]
        if want_reduced:
            down_ref = rest[0]
            rest = rest[1:]
        gate_ref, up_ref = rest[:2]
        rest = rest[2:]
        if fresh:
            prod_ref, act_ref, kept_gate, kept_up = rest[:4]
            rest = rest[4:]
        else:
            prod_ref, act_ref, kept_gate, kept_up = rest[4:8]
            rest = rest[8:]
        if want_reduced:
            reduced_ref = rest[0]
            rest = rest[1:]
        held, gate_in, up_in, prod_tile, act_tile, in_sem, kept_sem, stream_sem, out_sem = rest

        def kept_copies(t):
            col = pl.multiple_of(t * TILE, TILE)
            return [
                pltpu.make_async_copy(gate_ref.at[:, pl.ds(col, TILE)], kept_gate.at[t], kept_sem.at[0, t]),
                pltpu.make_async_copy(up_ref.at[:, pl.ds(col, TILE)], kept_up.at[t], kept_sem.at[1, t]),
            ]

        def stream_copies(s):
            col = pl.multiple_of((first_streamed + s) * TILE, TILE)
            slot = lax.rem(s, 2)
            return [
                pltpu.make_async_copy(gate_ref.at[:, pl.ds(col, TILE)], gate_in.at[slot], stream_sem.at[0, slot]),
                pltpu.make_async_copy(up_ref.at[:, pl.ds(col, TILE)], up_in.at[slot], stream_sem.at[1, slot]),
            ]

        def start(copies):
            for copy in copies:
                copy.start()

        def wait(copies):
            for copy in copies:
                copy.wait()

        core = meta_ref[0]
        arrivals = []
        for k in range(n_pieces):
            base, sibling, offset, length = places[k]
            side = (1 - core) if sibling else core
            row = pl.multiple_of(base + side * half + offset, 32)
            arrivals.append(pltpu.make_async_copy(piece_refs[k], held.at[pl.ds(row, length)], in_sem.at[k]))
        start(arrivals)
        if fresh:
            for t in range(n_kept):
                start(kept_copies(t))
        for s in range(min(2, n_streamed)):
            start(stream_copies(s))
        wait(arrivals)
        if want_reduced:
            found = lax.dot_general(held[...], down_ref[...], (((1,), (1,)), ((), ())), preferred_element_type=jnp.float32)
            for b in range(count):
                at = slice(b * block_len, (b + 1) * block_len)
                reduced_ref[at, :] = jnp.where(meta_ref[1 + 3 * (first + b) + 2] == 1, found[at], 0.0).astype(jnp.bfloat16)

        def out_copies(done, tile_at):
            slot = lax.rem(done, 2)
            col = pl.multiple_of(tile_at * TILE, TILE)
            made = []
            for b in range(count):
                block_row = pl.multiple_of(meta_ref[1 + 3 * (first + b)] * block_len, block_len)
                for n, (tile, out) in enumerate(((prod_tile, prod_ref), (act_tile, act_ref))):
                    made.append(pltpu.make_async_copy(
                        tile.at[slot, pl.ds(b * block_len, block_len)],
                        out.at[pl.ds(block_row, block_len), pl.ds(col, TILE)],
                        out_sem.at[slot, 2 * b + n]))
            return made

        def compute(done, tile_at, gate_tile, up_tile):
            @pl.when(done >= 2)
            def _():
                wait(out_copies(done - 2, tile_at))

            slot = lax.rem(done, 2)
            rows_in = held[...]
            gate_out = jnp.dot(rows_in, gate_tile, preferred_element_type=jnp.float32)
            up_out = jnp.dot(rows_in, up_tile, preferred_element_type=jnp.float32)
            for b in range(count):
                at = slice(b * block_len, (b + 1) * block_len)
                gate_part = gate_out[at]
                act = gate_part / (1.0 + jnp.exp(-gate_part))
                live = lax.broadcasted_iota(jnp.int32, act.shape, 0) < meta_ref[1 + 3 * (first + b) + 1]
                act_tile[slot, at, :] = jnp.where(live, act, 0.0).astype(jnp.bfloat16)
                prod_tile[slot, at, :] = jnp.where(live, act * up_out[at], 0.0).astype(jnp.bfloat16)
            start(out_copies(done, tile_at))

        if n_kept:
            def on_kept(t, carry):
                if fresh:
                    wait(kept_copies(t))
                compute(t, t, kept_gate[t], kept_up[t])
                return carry

            lax.fori_loop(0, n_kept, on_kept, 0)
        if n_streamed:
            def on_streamed(s, carry):
                wait(stream_copies(s))
                slot = lax.rem(s, 2)
                compute(n_kept + s, first_streamed + s, gate_in[slot], up_in[slot])

                @pl.when(s + 2 < n_streamed)
                def _():
                    start(stream_copies(s + 2))
                return carry

            lax.fori_loop(0, n_streamed, on_streamed, 0)
        total = n_kept + n_streamed
        for done in range(max(0, total - 2), total):
            wait(out_copies(done, 0))

    any_spec = pl.BlockSpec(memory_space=pl.ANY)
    vmem_spec = pl.BlockSpec(memory_space=pltpu.VMEM)
    in_specs = [any_spec] * n_pieces
    operands = [meta] + flat
    if want_reduced:
        in_specs.append(vmem_spec)
        operands.append(down)
    in_specs += [any_spec, any_spec]
    operands += [gate_matrix, up_matrix]
    result = jax.ShapeDtypeStruct((row_total, columns), jnp.bfloat16)
    out_specs = [any_spec, any_spec, vmem_spec, vmem_spec]
    out_shape = [result, result] + [pltpu.VMEM((KEPT, width, TILE), jnp.bfloat16)] * 2
    aliases = {}
    if not fresh:
        in_specs += [any_spec, any_spec, vmem_spec, vmem_spec]
        aliases = {len(operands) + k: k for k in range(4)}
        operands += list(earlier) + list(kept)
    if want_reduced:
        out_specs.append(vmem_spec)
        out_shape.append(jax.ShapeDtypeStruct((rows, rank), jnp.bfloat16))
    buffers = min(2, n_streamed) or 1
    stream_shape = (buffers, width, TILE) if n_streamed else (1, 16, 128)
    return pl.pallas_call(
        kernel,
        grid_spec=pltpu.PrefetchScalarGridSpec(
            num_scalar_prefetch=1,
            grid=(1,),
            in_specs=in_specs,
            out_specs=out_specs,
            scratch_shapes=[
                pltpu.VMEM((rows, width), jnp.bfloat16),
                pltpu.VMEM(stream_shape, jnp.bfloat16),
                pltpu.VMEM(stream_shape, jnp.bfloat16),
                pltpu.VMEM((2, rows, TILE), jnp.bfloat16),
                pltpu.VMEM((2, rows, TILE), jnp.bfloat16),
                pltpu.SemaphoreType.DMA((n_pieces,)),
                pltpu.SemaphoreType.DMA((2, KEPT)),
                pltpu.SemaphoreType.DMA((2, 2)),
                pltpu.SemaphoreType.DMA((2, 2 * count)),
            ],
        ),
        out_shape=out_shape,
        input_output_aliases=aliases,
        compiler_params=pltpu.CompilerParams(dimension_semantics=("arbitrary",), vmem_limit_bytes=VMEM_LIMIT),
        cost_estimate=pl.CostEstimate(
            flops=4 * rows * width * TILE * len(tiles),
            bytes_accessed=4 * width * TILE * (len(tiles) if fresh else n_streamed), transcendentals=0),
    )(*operands)


def place_call(meta, owned, row_total, block_len):
    rank = owned[0].shape[1]

    def kernel(*refs):
        meta_ref, table_ref = refs[0], refs[-1]
        table_ref[...] = jnp.zeros_like(table_ref)
        number = 0
        for ref in refs[1:-1]:
            for b in range(ref.shape[0] // block_len):
                row = pl.multiple_of(meta_ref[1 + 3 * number] * block_len, block_len)
                table_ref[pl.ds(row, block_len), :] = ref[b * block_len:(b + 1) * block_len, :]
                number += 1

    whole = pl.BlockSpec(memory_space=pltpu.VMEM)
    return pl.pallas_call(
        kernel,
        in_specs=[pl.BlockSpec(memory_space=pltpu.SMEM)] + [whole] * len(owned),
        out_specs=whole,
        out_shape=jax.ShapeDtypeStruct((row_total, rank), jnp.bfloat16),
        compiler_params=pltpu.CompilerParams(vmem_limit_bytes=4 * 1024 * 1024),
        cost_estimate=pl.CostEstimate(flops=0, bytes_accessed=1024 * 1024, transcendentals=0),
    )(meta, *owned)


def late_call(meta, first, pieces, down, owned, block_len):
    rank, width = down.shape
    half = block_len // 2
    n_pieces = len(pieces)

    def kernel(*refs):
        meta_ref = refs[0]
        piece_refs = refs[1:1 + n_pieces]
        down_ref, owned_ref, late_ref, held, in_sem = refs[1 + n_pieces:]
        core = meta_ref[0]
        copies = []
        for k, (piece, sibling, offset) in enumerate(pieces):
            side = (1 - core) if sibling else core
            row = pl.multiple_of(side * half + offset, 32)
            copies.append(pltpu.make_async_copy(piece_refs[k], held.at[pl.ds(row, piece.shape[0])], in_sem.at[k]))
        for copy in copies:
            copy.start()
        late_ref[:2 * block_len, :] = owned_ref[...]
        for copy in copies:
            copy.wait()
        found = lax.dot_general(held[...], down_ref[...], (((1,), (1,)), ((), ())), preferred_element_type=jnp.float32)
        late_ref[2 * block_len:, :] = jnp.where(meta_ref[1 + 3 * first + 2] == 1, found, 0.0).astype(jnp.bfloat16)

    whole = pl.BlockSpec(memory_space=pltpu.VMEM)
    return pl.pallas_call(
        kernel,
        in_specs=[pl.BlockSpec(memory_space=pltpu.SMEM)] + [pl.BlockSpec(memory_space=pl.ANY)] * n_pieces + [whole] * 2,
        out_specs=whole,
        out_shape=jax.ShapeDtypeStruct((3 * block_len, rank), jnp.bfloat16),
        scratch_shapes=[pltpu.VMEM((block_len, width), jnp.bfloat16), pltpu.SemaphoreType.DMA((n_pieces,))],
        compiler_params=pltpu.CompilerParams(vmem_limit_bytes=12 * 1024 * 1024),
        cost_estimate=pl.CostEstimate(flops=2 * block_len * width * 256, bytes_accessed=4 * 1024 * 1024, transcendentals=0),
    )(meta, *[piece for piece, _, _ in pieces], down, owned)


def finish_call(numbers, base, early, late, lowrank_up, prod, act, block_len):
    row_total, columns = prod.shape
    rank = early.shape[1]
    n_late = len(late)

    def kernel(*refs):
        numbers_ref, early_ref = refs[:2]
        late_refs = refs[2:2 + n_late]
        map_ref, prod_ref, act_ref, out_ref, entries = refs[2 + n_late:]
        b = pl.program_id(0)

        @pl.when(b == 0)
        def _():
            at = 0
            for ref in late_refs:
                entries[at:at + ref.shape[0], :] = ref[...]
                at += ref.shape[0]

        reduced = early_ref[...]
        for kind in range(3):
            row = pl.multiple_of(numbers_ref[base + 5 * b + 2 + kind] * block_len, block_len)
            reduced = reduced + entries[pl.ds(row, block_len), :]
        term = jnp.dot(reduced, map_ref[0], preferred_element_type=jnp.float32)
        total = prod_ref[...].astype(jnp.float32) + act_ref[...].astype(jnp.float32) * (lowrank_scale * term)
        live = lax.broadcasted_iota(jnp.int32, total.shape, 0) < numbers_ref[base + 5 * b + 1]
        out_ref[...] = jnp.where(live, total, 0.0).astype(jnp.bfloat16)

    row_spec = pl.BlockSpec((block_len, columns), lambda b, s: (b, 0))
    return pl.pallas_call(
        kernel,
        grid_spec=pltpu.PrefetchScalarGridSpec(
            num_scalar_prefetch=1,
            grid=(row_total // block_len,),
            in_specs=[pl.BlockSpec((block_len, rank), lambda b, s: (b, 0))]
            + [pl.BlockSpec(part.shape, lambda b, s: (0, 0)) for part in late]
            + [pl.BlockSpec((1, rank, columns), lambda b, s: (s[base + 5 * b], 0, 0)), row_spec, row_spec],
            out_specs=row_spec,
            scratch_shapes=[pltpu.VMEM((sum(part.shape[0] for part in late), rank), jnp.bfloat16)],
        ),
        out_shape=jax.ShapeDtypeStruct((row_total, columns), jnp.bfloat16),
        input_output_aliases={3 + n_late: 0},
        compiler_params=pltpu.CompilerParams(dimension_semantics=("arbitrary",), vmem_limit_bytes=16 * 1024 * 1024),
        cost_estimate=pl.CostEstimate(
            flops=2 * row_total * columns * 256, bytes_accessed=6 * row_total * columns, transcendentals=0),
    )(numbers, early, *late, lowrank_up, prod, act)


def on_ring(tokens, gate_matrix, up_matrix, lowrank_down, lowrank_up, tenant, adapter_storage_slot, live_count):
    block_count = tenant.shape[0]
    rows_here, width = tokens.shape
    chips = block_count
    block_len = 2 * rows_here
    row_total = block_count * block_len
    columns = gate_matrix.shape[1]
    me = lax.axis_index("tensor")
    core = lax.rem(me, 2)
    chip = me // 2

    def place_of(number):
        return jnp.where(lax.rem(number, 2) == 0, number // 2, chips - 1 - number // 2)

    def number_at(place):
        at = lax.rem(place + chips, chips)
        return jnp.where(at < chips // 2, 2 * at, 2 * (chips - 1 - at) + 1)

    order = jnp.array([0, -1, 1, -2, 2, -3, 3, -4], jnp.int32)
    numbers = number_at(place_of(chip) + order)
    slots = adapter_storage_slot[tenant]
    here = (slots == me).astype(jnp.int32)
    fields = jnp.stack([numbers, live_count[numbers], here[numbers]], axis=1).astype(jnp.int32)
    every = jnp.arange(block_count, dtype=jnp.int32)
    entry_of = [(number_at(place_of(every) + away) ^ chip) * 3 + kind for kind, away in enumerate((3, -3, 4))]
    last_fields = jnp.stack([slots, live_count] + entry_of, axis=1).astype(jnp.int32).reshape(-1)

    meta = jnp.concatenate([core[None].astype(jnp.int32), fields.reshape(-1), last_fields])
    last_at = 1 + fields.size

    right, left = ring_pairs(chips, 1), ring_pairs(chips, -1)

    def send(value, pairs):
        return lax.ppermute(value, "tensor", pairs)

    def flip(value, bits):
        return lax.ppermute(value, "tensor", [(d, d ^ bits) for d in range(2 * chips)])

    down = lowrank_down[0]
    weights = (gate_matrix, up_matrix)
    n_tiles = columns // TILE
    all_tiles = list(range(n_tiles))
    from_left, from_right = tokens, tokens
    blocks = [[(tokens, False, 0), (flip(tokens, 1), True, 0)]]
    state = (row_total, row_total)
    kept = None
    owned = []
    first = 0
    for step in range(3):
        from_left = send(from_left, right)
        from_right = send(from_right, left)
        out = pass_call(meta, first, blocks, down, *weights, kept, state, all_tiles, block_len, True)
        state = out[:2]
        kept = out[2:4]
        owned.append(out[-1])
        first += len(blocks)
        blocks = [[(v, False, 0), (flip(v, 1), True, 0)] for v in (from_left, from_right)]
    cut = rows_here // 2
    last_low = send(from_left[:cut], right)
    last_high = send(from_right[cut:], left)
    early = place_call(meta, owned, row_total, block_len)
    for bits in (1, 2, 4, 8):
        early = early + flip(early, bits)
    *state, kept_gate, kept_up, part = pass_call(
        meta, first, blocks, down, *weights, kept, state, all_tiles, block_len, True)
    kept = (kept_gate, kept_up)
    first += 2
    pieces = [
        (last_low, False, 0), (flip(last_low, 1), True, 0),
        (last_high, False, cut), (flip(last_high, 1), True, cut),
    ]
    mine = late_call(meta, first, pieces, down, part, block_len)
    on_chip = mine + flip(mine, 1)
    across = flip(mine, 2) + flip(mine, 3)
    both = jnp.concatenate([on_chip, across], axis=0)
    late = [both] + [flip(both, 4 * k) for k in range(1, chips // 2)]
    for tiles in (all_tiles[KEPT:], all_tiles[:KEPT]):
        out = pass_call(meta, first, [pieces], down, *weights, kept, state, tiles, block_len, False)
        state, kept = out[:2], out[2:]
    return finish_call(meta, last_at, early, late, lowrank_up, *state, block_len)


def on_device(
    tokens,
    gate_matrix,
    up_matrix,
    lowrank_down,
    lowrank_up,
    tenant,
    adapter_storage_slot,
    live_count,
):
    my_index = lax.axis_index("tensor")
    gathered = lax.all_gather(tokens, "tensor", axis=0, tiled=True)
    row_total = gathered.shape[0]
    width = gathered.shape[1]
    block_count = tenant.shape[0]
    block_len = row_total // block_count
    hidden_columns = gate_matrix.shape[1]
    gate_out = jnp.dot(gathered, gate_matrix, preferred_element_type=jnp.float32)
    up_output = jnp.dot(gathered, up_matrix, preferred_element_type=jnp.float32)
    slot_numbers = adapter_storage_slot[tenant]
    rows_block = gathered.reshape(block_count, block_len, width)
    per_replica = lowrank_down.shape[0]
    rank_width = lowrank_down.shape[1]
    first_slot = my_index * per_replica
    pieces = []
    for block in range(block_count):
        slot_here = slot_numbers[block]
        mine = jnp.logical_and(slot_here >= first_slot, slot_here < first_slot + per_replica)
        resident_slot = jnp.clip(slot_here - first_slot, 0, per_replica - 1)
        down_matrix = lax.dynamic_index_in_dim(lowrank_down, resident_slot, 0, keepdims=False)
        block_rows = rows_block[block]

        def product_fn(rows_in=block_rows, map_in=down_matrix):
            return lax.dot_general(
                rows_in, map_in, (((1,), (1,)), ((), ())), preferred_element_type=jnp.float32
            )

        def empty_fn():
            return jnp.zeros((block_len, rank_width), jnp.float32)

        pieces.append(lax.cond(mine, product_fn, empty_fn))
    partial_value = jnp.stack(pieces, axis=0)
    reduced_output = lax.psum(partial_value, "tensor").astype(jnp.bfloat16)
    every_slot = jnp.arange(lowrank_up.shape[0], dtype=jnp.int32)
    slot_indicator = (slot_numbers[:, None] == every_slot[None, :]).astype(jnp.bfloat16)
    adapter_up = jnp.einsum(
        "oe,exz->oxz", slot_indicator, lowrank_up, preferred_element_type=jnp.float32
    ).astype(jnp.bfloat16)
    lowrank_term = jnp.einsum(
        "who,wok->whk", reduced_output, adapter_up, preferred_element_type=jnp.float32
    )
    up_output = up_output + lowrank_scale * lowrank_term.reshape(row_total, hidden_columns)
    positions = jnp.arange(block_len, dtype=jnp.int32)
    live_rows = (positions[None, :] < live_count[:, None]).reshape(row_total, 1)
    hidden = jnp.where(live_rows, jax.nn.silu(gate_out) * up_output, 0.0)
    return hidden.astype(jnp.bfloat16)


def solution(mesh):
    placed = (
        P(("groups", "tensor"), None),
        P(None, "tensor"),
        P(None, "tensor"),
        P("tensor", None, None),
        P(None, None, "tensor"),
        P("groups"),
        P(),
        P("groups"),
    )
    run = on_ring if mesh.shape["tensor"] == 16 else on_device
    return jax.shard_map(
        run, mesh=mesh, in_specs=placed, out_specs=P("groups", "tensor"), check_vma=False
    )
```

time: 197 us -> 256 us (1.30)
  waiting for transfers between devices: 20.7 us -> 58.1 us
  Pallas kernels: 150 us -> 159 us
  starting transfers between devices: 16 us -> 21.9 us
  local copies, waits for them, and re-layouts: 6.08 us -> 11.3 us
    ppermute x0 -> x19, waiting for transfers between devices: none -> 39 us  [flip(): lax.ppermute(value, 'tensor', [(d, d ^ bits) for d in range(2 * chips)])]
    ppermute x0 -> x19, starting transfers between devices: none -> 13.4 us  [flip(): lax.ppermute(value, 'tensor', [(d, d ^ bits) for d in range(2 * chips)])]
    pallas_call x8 -> x6, Pallas kernels: 140 us -> 149 us  [pass_call(): pl.pallas_call(kernel, grid_spec=pltpu.PrefetchScalarGridSpec(num_scalar_...]
    ppermute x21 -> x8, starting transfers between devices: 16 us -> 8.55 us  [send(): return lax.ppermute(value, 'tensor', pairs)]
    unnamed x12 -> x50, local copies, waits for them, and re-layouts: 2.47 us -> 7.61 us
    ppermute x21 -> x8, waiting for transfers between devices: 20.7 us -> 19.1 us  [send(): return lax.ppermute(value, 'tensor', pairs)]
  transfers between devices with their start and end apart: 21 -> 27, of which waited for: 2 -> 5; matrix products, arithmetic and copies ran while one was open for 3% -> 2% of each run, Pallas kernels for 72% -> 59%
where the time goes in v2:
time: 256 us; the launch traced here: 253 us
  Pallas kernels  159 us (62%)
  waiting for transfers between devices  58.1 us (23%)
  starting transfers between devices  21.9 us (9%)
  local copies, waits for them, and re-layouts  11.3 us (4%)
    pallas_call x6, Pallas kernels, pass_call(): pl.pallas_call(kernel, grid_spec=pltpu.PrefetchScalarGridSpec(num_scalar_...  149 us
    ppermute x19, waiting for transfers between devices, flip(): lax.ppermute(value, 'tensor', [(d, d ^ bits) for d in range(2 * chips)])  39 us
    ppermute x8, waiting for transfers between devices, send(): return lax.ppermute(value, 'tensor', pairs)  19.1 us
    ppermute x19, starting transfers between devices, flip(): lax.ppermute(value, 'tensor', [(d, d ^ bits) for d in range(2 * chips)])  13.4 us
    ppermute x8, starting transfers between devices, send(): return lax.ppermute(value, 'tensor', pairs)  8.55 us
    pallas_call x1, Pallas kernels, finish_call(): pl.pallas_call(kernel, grid_spec=pltpu.PrefetchScalarGridSpec(num_scalar_...  8.11 us
    unnamed x50, local copies, waits for them, and re-layouts  7.61 us
  transfers between devices with their start and end apart: 27, of which 5 were waited for; matrix products, arithmetic and copies ran while one was open for 2% of the time, Pallas kernels for 59%

profile of v2, /device:TPU:4, one launch (start us, length us, event | category | flops | bytes accessed | tf_op | source)
XLA Modules:
  0.0 253.1 jit_solution(16677331149685764126)
XLA Ops:
  0.0 1.6 collective-permute-start.1
  1.6 0.4 collective-permute-start.3
  2.0 0.7 compare_select_fusion.1
  2.7 1.3 gather_fusion
  4.0 0.7 compare_select_fusion
  4.7 0.6 gather_fusion.1
  5.3 0.6 gather_fusion.2
  6.0 19.1 %collective-permute-done.1.refs_1_ = bf16[64,8192]{1,0:T(8,128)(2,1)S(1)} collective-permute-done((bf16[64,8192]{1,0:T(8,128)(2,1)}, bf16[64,8192]{1,0:T(8,128)(2,1)S(1)}, u32[]{:S(2)}, u32[]{:S(2)}) %collective-permute-start.1) | collective-permute-done | bytes 1048608 | tf_op jit(solution)/shard_map/ppermute | solution.py:355
  25.1 1.6 collective-permute-start.5
  26.7 0.2 collective-permute-start.4
  26.9 0.4 collective-permute-start.7
  27.6 0.7 stack.30
  28.4 0.7 pad_add_fusion.1.refs_0_
  29.1 1.0 copy-done.20
  30.1 29.5 %shard_map.91 = (bf16[1024,1792]{1,0:T(8,128)(2,1)}, bf16[1024,1792]{1,0:T(8,128)(2,1)}, bf16[3,8192,256]{2,1,0:T(8,128)(2,1)S(1)}, bf16[3,8192,256]{2,1,0:T(8,128)(2,1)S(1)}, bf16[128,64]{1,0:T(8,128)(2,1)}) custom-call(s32[65]{0:T(128)} %pad_add_fusion.1.refs_0_, bf16[64,8192]{1,0:T(8,128)(2,1)} %refs_1_.1, bf16[64,8192]{1,0:T(8,128)(2,1)} %copy-done.20, ...), custom_call_target="tpu_custom_call" | custom-call | flops 7516192768 | bytes 58720256 | tf_op jit(solution)/shard_map/pallas_call | solution.py:188
  59.7 1.6 collective-permute-start.13
  61.3 0.2 collective-permute-start.8
  61.5 0.5 collective-permute-start.16
  62.0 31.6 %shard_map.92 = (bf16[1024,1792]{1,0:T(8,128)(2,1)}, bf16[1024,1792]{1,0:T(8,128)(2,1)}, bf16[3,8192,256]{2,1,0:T(8,128)(2,1)S(1)}, bf16[3,8192,256]{2,1,0:T(8,128)(2,1)S(1)}, bf16[256,64]{1,0:T(8,128)(2,1)}) custom-call(s32[65]{0:T(128)} %pad_add_fusion.1.refs_0_, ...), custom_call_target="tpu_custom_call", output_to_operand_aliasing={{0}: (8, {}), {1}: (9, {}), {2}: (10, {}), {3}: (11, {})} | custom-call | flops 15032385536 | bytes 33554432 | tf_op jit(solution)/shard_map/pallas_call | solution.py:188
  93.7 0.5 collective-permute-start.20
  94.2 1.1 copy-done.23
  95.3 0.3 copy-done.24
  95.7 31.6 %shard_map.93 = (bf16[1024,1792]{1,0:T(8,128)(2,1)}, bf16[1024,1792]{1,0:T(8,128)(2,1)}, bf16[3,8192,256]{2,1,0:T(8,128)(2,1)S(1)}, bf16[3,8192,256]{2,1,0:T(8,128)(2,1)S(1)}, bf16[256,64]{1,0:T(8,128)(2,1)}) custom-call(s32[65]{0:T(128)} %pad_add_fusion.1.refs_0_, ...), custom_call_target="tpu_custom_call", output_to_operand_aliasing={{0}: (8, {}), {1}: (9, {}), {2}: (10, {}), {3}: (11, {})} | custom-call | flops 15032385536 | bytes 33554432 | tf_op jit(solution)/shard_map/pallas_call | solution.py:188
  127.3 0.8 copy-done.11
  128.2 0.6 shard_map.94
  129.0 1.6 collective-permute-start.14
  130.7 0.7 collective-permute-start.17
  131.5 1.5 collective-permute-start.10
  133.0 15.9 %collective-permute-done.10 = bf16[1024,64]{1,0:T(8,128)(2,1)S(1)} collective-permute-done((bf16[1024,64]{1,0:T(8,128)(2,1)S(1)}, bf16[1024,64]{1,0:T(8,128)(2,1)S(1)}, u32[]{:S(2)}, u32[]{:S(2)}) %collective-permute-start.10) | collective-permute-done | bytes 131104 | tf_op jit(solution)/shard_map/ppermute | solution.py:358
  149.1 7.8 %collective-permute-done.11 = bf16[1024,64]{1,0:T(8,128)(2,1)S(1)} collective-permute-done((bf16[1024,64]{1,0:T(8,128)(2,1)S(1)}, bf16[1024,64]{1,0:T(8,128)(2,1)S(1)}, u32[]{:S(2)}, u32[]{:S(2)}) %collective-permute-start.11) | collective-permute-done | bytes 131104 | tf_op jit(solution)/shard_map/ppermute | solution.py:358
  157.0 3.7 %collective-permute-start.12 = (bf16[1024,64]{1,0:T(8,128)(2,1)S(1)}, bf16[1024,64]{1,0:T(8,128)(2,1)S(1)}, u32[]{:S(2)}, u32[]{:S(2)}) collective-permute-start(bf16[1024,64]{1,0:T(8,128)(2,1)S(1)} %add.169), channel_id=1, source_target_pairs={{0,8},{1,9},{2,10},{3,11},{4,12},{5,13},{6,14},{7,15},{8,0},{9,1},... | collective-permute-start | bytes 393224 | tf_op jit(solution)/shard_map/ppermute | solution.py:358
  160.7 0.5 collective-permute-start.18
  161.2 10.3 %collective-permute-done.12 = bf16[1024,64]{1,0:T(8,128)(2,1)S(1)} collective-permute-done((bf16[1024,64]{1,0:T(8,128)(2,1)S(1)}, bf16[1024,64]{1,0:T(8,128)(2,1)S(1)}, u32[]{:S(2)}, u32[]{:S(2)}) %collective-permute-start.12) | collective-permute-done | bytes 131104 | tf_op jit(solution)/shard_map/ppermute | solution.py:358
  171.6 1.0 copy-done.21
  172.6 0.4 copy-done.22
  172.9 31.7 %shard_map.95 = (bf16[1024,1792]{1,0:T(8,128)(2,1)}, bf16[1024,1792]{1,0:T(8,128)(2,1)}, bf16[3,8192,256]{2,1,0:T(8,128)(2,1)S(1)}, bf16[3,8192,256]{2,1,0:T(8,128)(2,1)S(1)}, bf16[256,64]{1,0:T(8,128)(2,1)}) custom-call(s32[65]{0:T(128)} %pad_add_fusion.1.refs_0_, ...), custom_call_target="tpu_custom_call", output_to_operand_aliasing={{0}: (8, {}), {1}: (9, {}), {2}: (10, {}), {3}: (11, {})} | custom-call | flops 15032385536 | bytes 33554432 | tf_op jit(solution)/shard_map/pallas_call | solution.py:188
  204.8 0.9 copy-done.9
  205.7 1.4 shard_map.96
  207.2 0.7 collective-permute-start.22
  207.9 1.1 collective-permute-start.23
  209.1 15.4 %shard_map.97 = (bf16[1024,1792]{1,0:T(8,128)(2,1)}, bf16[1024,1792]{1,0:T(8,128)(2,1)}, bf16[3,8192,256]{2,1,0:T(8,128)(2,1)S(1)}, bf16[3,8192,256]{2,1,0:T(8,128)(2,1)S(1)}) custom-call(s32[65]{0:T(128)} %pad_add_fusion.1.refs_0_, bf16[32,8192]{1,0:T(8,128)(2,1)} %copy-done.4, ...), custom_call_target="tpu_custom_call", output_to_operand_aliasing={{0}: (7, {}), {1}: (8, {}), {2}: (9, {}), {3}: (10, {})} | custom-call | flops 4294967296 | bytes 33554432 | tf_op jit(solution)/shard_map/pallas_call | solution.py:188
  224.6 0.8 collective-permute-start.24
  225.4 3.4 %collective-permute-start.25 = (bf16[768,64]{1,0:T(8,128)(2,1)S(1)}, bf16[768,64]{1,0:T(8,128)(2,1)S(1)}, u32[]{:S(2)}, u32[]{:S(2)}) collective-permute-start(bf16[768,64]{1,0:T(8,128)(2,1)S(1)} %pad_maximum_fusion.refs_2_), channel_id=1, source_target_pairs={{0,8},{1,9},{2,10},{3,11},{4,12},{5,13},{6,14},{7,15},{8,0},{9,1},... | collective-permute-start | bytes 294920 | tf_op jit(solution)/shard_map/ppermute | solution.py:358
  228.8 0.3 collective-permute-start.26
  229.1 8.9 %shard_map.98 = (bf16[1024,1792]{1,0:T(8,128)(2,1)}, bf16[1024,1792]{1,0:T(8,128)(2,1)}, bf16[3,8192,256]{2,1,0:T(8,128)(2,1)S(1)}, bf16[3,8192,256]{2,1,0:T(8,128)(2,1)S(1)}) custom-call(s32[65]{0:T(128)} %pad_add_fusion.1.refs_0_, bf16[32,8192]{1,0:T(8,128)(2,1)} %copy-done.4, ...), custom_call_target="tpu_custom_call", output_to_operand_aliasing={{0}: (7, {}), {1}: (8, {}), {2}: (9, {}), {3}: (10, {})} | custom-call | flops 3221225472 | tf_op jit(solution)/shard_map/pallas_call | solution.py:188
  238.0 4.9 %collective-permute-done.25.refs_4_ = bf16[768,64]{1,0:T(8,128)(2,1)S(1)} collective-permute-done((bf16[768,64]{1,0:T(8,128)(2,1)S(1)}, bf16[768,64]{1,0:T(8,128)(2,1)S(1)}, u32[]{:S(2)}, u32[]{:S(2)}) %collective-permute-start.25) | collective-permute-done | bytes 98336 | tf_op jit(solution)/shard_map/ppermute | solution.py:358
  243.0 2.0 copy-done.2
  245.0 8.1 %shard_map.99 = bf16[1024,1792]{1,0:T(8,128)(2,1)} custom-call(s32[65]{0:T(128)S(1)} %copy-done.14, bf16[1024,64]{1,0:T(8,128)(2,1)S(1)} %add.170.refs_1_, bf16[768,64]{1,0:T(8,128)(2,1)S(1)} %pad_maximum_fusion.refs_2_, bf16[768,64]{1,0:T(8,128)(2,1)S(1)} %collective-permute-done.24.refs_3_, ...), custom_call_target="tpu_custom_call", output_to_operand_aliasing={{}: (7, {})} | custom-call | flops 939524096 | bytes 11010048 | tf_op jit(solution)/shard_map/pallas_call | solution.py:303
  (91 shorter events, 1.5 us)
Async XLA Ops:
  0.0 4.7 %copy-start = (s32[16]{0:T(128)S(1)}, s32[16]{0:T(128)}, u32[]{:S(2)}) copy-start(s32[16]{0:T(128)} %param.15) | copy-start | bytes 196
  0.0 25.1 %collective-permute-start.1 = (bf16[64,8192]{1,0:T(8,128)(2,1)}, bf16[64,8192]{1,0:T(8,128)(2,1)S(1)}, u32[]{:S(2)}, u32[]{:S(2)}) collective-permute-start(bf16[64,8192]{1,0:T(8,128)(2,1)} %refs_1_.1), channel_id=1, source_target_pairs={{0,4},{1,5},{4,8},{5,9},{8,12},{9,13},{12,14},{13,15},{14,10},{15,... | collective-permute-start | bytes 3145736 | tf_op jit(solution)/shard_map/ppermute | solution.py:355
  1.6 25.1 %collective-permute-start.3 = (bf16[64,8192]{1,0:T(8,128)(2,1)}, bf16[64,8192]{1,0:T(8,128)(2,1)S(1)}, u32[]{:S(2)}, u32[]{:S(2)}) collective-permute-start(bf16[64,8192]{1,0:T(8,128)(2,1)} %refs_1_.1), channel_id=1, source_target_pairs={{0,2},{1,3},{4,0},{5,1},{8,4},{9,5},{12,8},{13,9},{14,12},{15,13},... | collective-permute-start | bytes 3145736 | tf_op jit(solution)/shard_map/ppermute | solution.py:355
  2.0 27.1 %collective-permute-start = (bf16[64,8192]{1,0:T(8,128)(2,1)}, bf16[64,8192]{1,0:T(8,128)(2,1)S(1)}, u32[]{:S(2)}, u32[]{:S(2)}) collective-permute-start(bf16[64,8192]{1,0:T(8,128)(2,1)} %refs_1_.1), channel_id=1, source_target_pairs={{0,1},{1,0},{2,3},{3,2},{4,5},{5,4},{6,7},{7,6},{8,9},{9,8},{10,11... | collective-permute-start | bytes 3145736 | tf_op jit(solution)/shard_map/ppermute | solution.py:358
  25.1 34.5 %copy-start.18 = (bf16[64,8192]{1,0:T(8,128)(2,1)}, bf16[64,8192]{1,0:T(8,128)(2,1)S(1)}, u32[]{:S(2)}) copy-start(bf16[64,8192]{1,0:T(8,128)(2,1)S(1)} %collective-permute-done.1.refs_1_) | copy-start | bytes 3145732
  25.1 36.4 %collective-permute-start.2 = (bf16[64,8192]{1,0:T(8,128)(2,1)S(1)}, bf16[64,8192]{1,0:T(8,128)(2,1)}, u32[]{:S(2)}, u32[]{:S(2)}) collective-permute-start(bf16[64,8192]{1,0:T(8,128)(2,1)S(1)} %collective-permute-done.1.refs_1_), channel_id=1, source_target_pairs={{0,1},{1,0},{2,3},{3,2},{4,5},{5,4},{6,7},{7,6},{8,9},{9,8},{10,11... | collective-permute-start | bytes 3145736 | tf_op jit(solution)/shard_map/ppermute | solution.py:358
  25.1 34.5 %collective-permute-start.5 = (bf16[64,8192]{1,0:T(8,128)(2,1)S(1)}, bf16[64,8192]{1,0:T(8,128)(2,1)}, u32[]{:S(2)}, u32[]{:S(2)}) collective-permute-start(bf16[64,8192]{1,0:T(8,128)(2,1)S(1)} %collective-permute-done.1.refs_1_), channel_id=1, source_target_pairs={{0,4},{1,5},{4,8},{5,9},{8,12},{9,13},{12,14},{13,15},{14,10},{15,... | collective-permute-start | bytes 3145736 | tf_op jit(solution)/shard_map/ppermute | solution.py:355
  26.7 32.9 %copy-start.19 = (bf16[64,8192]{1,0:T(8,128)(2,1)}, bf16[64,8192]{1,0:T(8,128)(2,1)S(1)}, u32[]{:S(2)}) copy-start(bf16[64,8192]{1,0:T(8,128)(2,1)S(1)} %collective-permute-done.3.refs_3_) | copy-start | bytes 3145732
  26.7 35.3 %collective-permute-start.4 = (bf16[64,8192]{1,0:T(8,128)(2,1)S(1)}, bf16[64,8192]{1,0:T(8,128)(2,1)}, u32[]{:S(2)}, u32[]{:S(2)}) collective-permute-start(bf16[64,8192]{1,0:T(8,128)(2,1)S(1)} %collective-permute-done.3.refs_3_), channel_id=1, source_target_pairs={{0,1},{1,0},{2,3},{3,2},{4,5},{5,4},{6,7},{7,6},{8,9},{9,8},{10,11... | collective-permute-start | bytes 3145736 | tf_op jit(solution)/shard_map/ppermute | solution.py:358
  26.9 34.4 %collective-permute-start.7 = (bf16[64,8192]{1,0:T(8,128)(2,1)S(1)}, bf16[64,8192]{1,0:T(8,128)(2,1)}, u32[]{:S(2)}, u32[]{:S(2)}) collective-permute-start(bf16[64,8192]{1,0:T(8,128)(2,1)S(1)} %collective-permute-done.3.refs_3_), channel_id=1, source_target_pairs={{0,2},{1,3},{4,0},{5,1},{8,4},{9,5},{12,8},{13,9},{14,12},{15,13},... | collective-permute-start | bytes 3145736 | tf_op jit(solution)/shard_map/ppermute | solution.py:355
  59.6 34.6 %collective-permute-start.6 = (bf16[64,8192]{1,0:T(8,128)(2,1)}, bf16[64,8192]{1,0:T(8,128)(2,1)S(1)}, u32[]{:S(2)}, u32[]{:S(2)}) collective-permute-start(bf16[64,8192]{1,0:T(8,128)(2,1)} %collective-permute-done.5.refs_1_), channel_id=1, source_target_pairs={{0,1},{1,0},{2,3},{3,2},{4,5},{5,4},{6,7},{7,6},{8,9},{9,8},{10,11... | collective-permute-start | bytes 3145736 | tf_op jit(solution)/shard_map/ppermute | solution.py:358
  59.7 33.9 %collective-permute-start.13 = (bf16[64,8192]{1,0:T(8,128)(2,1)}, bf16[64,8192]{1,0:T(8,128)(2,1)S(1)}, u32[]{:S(2)}, u32[]{:S(2)}) collective-permute-start(bf16[64,8192]{1,0:T(8,128)(2,1)} %collective-permute-done.5.refs_1_), channel_id=1, source_target_pairs={{0,4},{1,5},{4,8},{5,9},{8,12},{9,13},{12,14},{13,15},{14,10},{15,... | collective-permute-start | bytes 3145736 | tf_op jit(solution)/shard_map/ppermute | solution.py:355
  61.3 32.9 %collective-permute-start.8 = (bf16[64,8192]{1,0:T(8,128)(2,1)}, bf16[64,8192]{1,0:T(8,128)(2,1)S(1)}, u32[]{:S(2)}, u32[]{:S(2)}) collective-permute-start(bf16[64,8192]{1,0:T(8,128)(2,1)} %collective-permute-done.7.refs_3_), channel_id=1, source_target_pairs={{0,1},{1,0},{2,3},{3,2},{4,5},{5,4},{6,7},{7,6},{8,9},{9,8},{10,11... | collective-permute-start | bytes 3145736 | tf_op jit(solution)/shard_map/ppermute | solution.py:358
  61.5 32.2 %collective-permute-start.16 = (bf16[64,8192]{1,0:T(8,128)(2,1)}, bf16[64,8192]{1,0:T(8,128)(2,1)S(1)}, u32[]{:S(2)}, u32[]{:S(2)}) collective-permute-start(bf16[64,8192]{1,0:T(8,128)(2,1)} %collective-permute-done.7.refs_3_), channel_id=1, source_target_pairs={{0,2},{1,3},{4,0},{5,1},{8,4},{9,5},{12,8},{13,9},{14,12},{15,13},... | collective-permute-start | bytes 3145736 | tf_op jit(solution)/shard_map/ppermute | solution.py:355
  93.6 35.3 %copy-start.16 = (bf16[64,8192]{1,0:T(8,128)(2,1)}, bf16[64,8192]{1,0:T(8,128)(2,1)S(1)}, u32[]{:S(2)}) copy-start(bf16[64,8192]{1,0:T(8,128)(2,1)S(1)} %collective-permute-done.13.refs_1_) | copy-start | bytes 3145732
  93.6 77.9 %collective-permute-start.19 = (bf16[64,8192]{1,0:T(8,128)(2,1)S(1)}, bf16[64,8192]{1,0:T(8,128)(2,1)S(1)}, u32[]{:S(2)}, u32[]{:S(2)}) collective-permute-start(bf16[64,8192]{1,0:T(8,128)(2,1)S(1)} %collective-permute-done.13.refs_1_), channel_id=1, source_target_pairs={{0,1},{1,0},{2,3},{3,2},{4,5},{5,4},{6,7},{7,6},{8,9},{9,8},{10,11... | collective-permute-start | bytes 3145736 | tf_op jit(solution)/shard_map/ppermute | solution.py:358
  93.7 36.9 %copy-start.17 = (bf16[64,8192]{1,0:T(8,128)(2,1)}, bf16[64,8192]{1,0:T(8,128)(2,1)S(1)}, u32[]{:S(2)}) copy-start(bf16[64,8192]{1,0:T(8,128)(2,1)S(1)} %collective-permute-done.16.refs_3_) | copy-start | bytes 3145732
  93.7 77.9 %collective-permute-start.20 = (bf16[64,8192]{1,0:T(8,128)(2,1)S(1)}, bf16[64,8192]{1,0:T(8,128)(2,1)S(1)}, u32[]{:S(2)}, u32[]{:S(2)}) collective-permute-start(bf16[64,8192]{1,0:T(8,128)(2,1)S(1)} %collective-permute-done.16.refs_3_), channel_id=1, source_target_pairs={{0,1},{1,0},{2,3},{3,2},{4,5},{5,4},{6,7},{7,6},{8,9},{9,8},{10,11... | collective-permute-start | bytes 3145736 | tf_op jit(solution)/shard_map/ppermute | solution.py:358
  94.2 1.1 copy-start.23
  94.2 1.5 copy-start.24
  95.7 31.6 %copy-start.10 = (bf16[256,64]{1,0:T(8,128)(2,1)S(1)}, bf16[256,64]{1,0:T(8,128)(2,1)}, u32[]{:S(2)}) copy-start(bf16[256,64]{1,0:T(8,128)(2,1)} %get-tuple-element.36.refs_2_) | copy-start | bytes 98308
  95.7 31.6 %copy-start.12 = (s32[65]{0:T(128)S(1)}, s32[65]{0:T(128)}, u32[]{:S(2)}) copy-start(s32[65]{0:T(128)} %pad_add_fusion.1.refs_0_) | copy-start | bytes 784
  95.7 31.7 %copy-start.15 = (bf16[128,64]{1,0:T(8,128)(2,1)S(1)}, bf16[128,64]{1,0:T(8,128)(2,1)}, u32[]{:S(2)}) copy-start(bf16[128,64]{1,0:T(8,128)(2,1)} %get-tuple-element.31.refs_1_) | copy-start | bytes 49156
  128.8 2.6 %collective-permute-start.9 = (bf16[1024,64]{1,0:T(8,128)(2,1)S(1)}, bf16[1024,64]{1,0:T(8,128)(2,1)S(1)}, u32[]{:S(2)}, u32[]{:S(2)}) collective-permute-start(bf16[1024,64]{1,0:T(8,128)(2,1)S(1)} %shard_map.94), channel_id=1, source_target_pairs={{0,1},{1,0},{2,3},{3,2},{4,5},{5,4},{6,7},{7,6},{8,9},{9,8},{10,11... | collective-permute-start | bytes 393224 | tf_op jit(solution)/shard_map/ppermute | solution.py:358
  129.0 31.7 %collective-permute-start.14 = (bf16[32,8192]{1,0:T(8,128)(2,1)S(1)}, bf16[32,8192]{1,0:T(8,128)(2,1)S(1)}, u32[]{:S(2)}, u32[]{:S(2)}) collective-permute-start(bf16[32,8192]{1,0:T(8,128)(2,1)S(1)} %slice.14), channel_id=1, source_target_pairs={{0,4},{1,5},{4,8},{5,9},{8,12},{9,13},{12,14},{13,15},{14,10},{15,... | collective-permute-start | bytes 1572872 | tf_op jit(solution)/shard_map/ppermute | solution.py:355
  130.7 30.0 %collective-permute-start.17 = (bf16[32,8192]{1,0:T(8,128)(2,1)S(1)}, bf16[32,8192]{1,0:T(8,128)(2,1)S(1)}, u32[]{:S(2)}, u32[]{:S(2)}) collective-permute-start(bf16[32,8192]{1,0:T(8,128)(2,1)S(1)} %slice.15), channel_id=1, source_target_pairs={{0,2},{1,3},{4,0},{5,1},{8,4},{9,5},{12,8},{13,9},{14,12},{15,13},... | collective-permute-start | bytes 1572872 | tf_op jit(solution)/shard_map/ppermute | solution.py:355
  131.5 17.5 %collective-permute-start.10 = (bf16[1024,64]{1,0:T(8,128)(2,1)S(1)}, bf16[1024,64]{1,0:T(8,128)(2,1)S(1)}, u32[]{:S(2)}, u32[]{:S(2)}) collective-permute-start(bf16[1024,64]{1,0:T(8,128)(2,1)S(1)} %add.167), channel_id=1, source_target_pairs={{0,2},{1,3},{2,0},{3,1},{4,6},{5,7},{6,4},{7,5},{8,10},{9,11},{10,... | collective-permute-start | bytes 393224 | tf_op jit(solution)/shard_map/ppermute | solution.py:358
  149.0 7.9 %collective-permute-start.11 = (bf16[1024,64]{1,0:T(8,128)(2,1)S(1)}, bf16[1024,64]{1,0:T(8,128)(2,1)S(1)}, u32[]{:S(2)}, u32[]{:S(2)}) collective-permute-start(bf16[1024,64]{1,0:T(8,128)(2,1)S(1)} %add.168), channel_id=1, source_target_pairs={{0,4},{1,5},{2,6},{3,7},{4,0},{5,1},{6,2},{7,3},{8,12},{9,13},{10,... | collective-permute-start | bytes 393224 | tf_op jit(solution)/shard_map/ppermute | solution.py:358
  157.0 14.5 %collective-permute-start.12 = (bf16[1024,64]{1,0:T(8,128)(2,1)S(1)}, bf16[1024,64]{1,0:T(8,128)(2,1)S(1)}, u32[]{:S(2)}, u32[]{:S(2)}) collective-permute-start(bf16[1024,64]{1,0:T(8,128)(2,1)S(1)} %add.169), channel_id=1, source_target_pairs={{0,8},{1,9},{2,10},{3,11},{4,12},{5,13},{6,14},{7,15},{8,0},{9,1},... | collective-permute-start | bytes 393224 | tf_op jit(solution)/shard_map/ppermute | solution.py:358
  160.7 44.0 %copy-start.4 = (bf16[32,8192]{1,0:T(8,128)(2,1)}, bf16[32,8192]{1,0:T(8,128)(2,1)S(1)}, u32[]{:S(2)}) copy-start(bf16[32,8192]{1,0:T(8,128)(2,1)S(1)} %collective-permute-done.14.refs_1_) | copy-start | bytes 1572868
  160.7 44.0 %collective-permute-start.15 = (bf16[32,8192]{1,0:T(8,128)(2,1)S(1)}, bf16[32,8192]{1,0:T(8,128)(2,1)S(1)}, u32[]{:S(2)}, u32[]{:S(2)}) collective-permute-start(bf16[32,8192]{1,0:T(8,128)(2,1)S(1)} %collective-permute-done.14.refs_1_), channel_id=1, source_target_pairs={{0,1},{1,0},{2,3},{3,2},{4,5},{5,4},{6,7},{7,6},{8,9},{9,8},{10,11... | collective-permute-start | bytes 1572872 | tf_op jit(solution)/shard_map/ppermute | solution.py:358
  160.7 44.0 %copy-start.5 = (bf16[32,8192]{1,0:T(8,128)(2,1)}, bf16[32,8192]{1,0:T(8,128)(2,1)S(1)}, u32[]{:S(2)}) copy-start(bf16[32,8192]{1,0:T(8,128)(2,1)S(1)} %collective-permute-done.17.refs_3_) | copy-start | bytes 1572868
  160.7 44.0 %collective-permute-start.18 = (bf16[32,8192]{1,0:T(8,128)(2,1)S(1)}, bf16[32,8192]{1,0:T(8,128)(2,1)S(1)}, u32[]{:S(2)}, u32[]{:S(2)}) collective-permute-start(bf16[32,8192]{1,0:T(8,128)(2,1)S(1)} %collective-permute-done.17.refs_3_), channel_id=1, source_target_pairs={{0,1},{1,0},{2,3},{3,2},{4,5},{5,4},{6,7},{7,6},{8,9},{9,8},{10,11... | collective-permute-start | bytes 1572872 | tf_op jit(solution)/shard_map/ppermute | solution.py:358
  171.6 1.3 copy-start.22
  172.9 31.8 %copy-start.3 = (bf16[1,64,8192]{2,1,0:T(8,128)(2,1)S(1)}, bf16[1,64,8192]{2,1,0:T(8,128)(2,1)}, u32[]{:S(2)}) copy-start(bf16[1,64,8192]{2,1,0:T(8,128)(2,1)} %param.12) | copy-start | bytes 3145732
  172.9 31.8 %copy-start.13 = (s32[65]{0:T(128)S(1)}, s32[65]{0:T(128)}, u32[]{:S(2)}) copy-start(s32[65]{0:T(128)} %pad_add_fusion.1.refs_0_) | copy-start | bytes 784
  204.7 4.4 %copy-start.6 = (bf16[32,8192]{1,0:T(8,128)(2,1)}, bf16[32,8192]{1,0:T(8,128)(2,1)S(1)}, u32[]{:S(2)}) copy-start(bf16[32,8192]{1,0:T(8,128)(2,1)S(1)} %collective-permute-done.15.refs_2_) | copy-start | bytes 1572868
  204.7 4.4 %copy-start.7 = (bf16[32,8192]{1,0:T(8,128)(2,1)}, bf16[32,8192]{1,0:T(8,128)(2,1)S(1)}, u32[]{:S(2)}) copy-start(bf16[32,8192]{1,0:T(8,128)(2,1)S(1)} %collective-permute-done.18.refs_4_) | copy-start | bytes 1572868
  207.1 17.4 %collective-permute-start.21 = (bf16[384,64]{1,0:T(8,128)(2,1)S(1)}, bf16[384,64]{1,0:T(8,128)(2,1)S(1)}, u32[]{:S(2)}, u32[]{:S(2)}) collective-permute-start(bf16[384,64]{1,0:T(8,128)(2,1)S(1)} %shard_map.96), channel_id=1, source_target_pairs={{0,1},{1,0},{2,3},{3,2},{4,5},{5,4},{6,7},{7,6},{8,9},{9,8},{10,11... | collective-permute-start | bytes 147464 | tf_op jit(solution)/shard_map/ppermute | solution.py:358
  207.2 17.3 %collective-permute-start.22 = (bf16[384,64]{1,0:T(8,128)(2,1)S(1)}, bf16[384,64]{1,0:T(8,128)(2,1)S(1)}, u32[]{:S(2)}, u32[]{:S(2)}) collective-permute-start(bf16[384,64]{1,0:T(8,128)(2,1)S(1)} %shard_map.96), channel_id=1, source_target_pairs={{0,2},{1,3},{2,0},{3,1},{4,6},{5,7},{6,4},{7,5},{8,10},{9,11},{10,... | collective-permute-start | bytes 147464 | tf_op jit(solution)/shard_map/ppermute | solution.py:358
  207.9 16.6 %collective-permute-start.23 = (bf16[384,64]{1,0:T(8,128)(2,1)S(1)}, bf16[384,64]{1,0:T(8,128)(2,1)S(1)}, u32[]{:S(2)}, u32[]{:S(2)}) collective-permute-start(bf16[384,64]{1,0:T(8,128)(2,1)S(1)} %shard_map.96), channel_id=1, source_target_pairs={{0,3},{1,2},{2,1},{3,0},{4,7},{5,6},{6,5},{7,4},{8,11},{9,10},{10,... | collective-permute-start | bytes 147464 | tf_op jit(solution)/shard_map/ppermute | solution.py:358
  224.6 13.4 %collective-permute-start.24 = (bf16[768,64]{1,0:T(8,128)(2,1)S(1)}, bf16[768,64]{1,0:T(8,128)(2,1)S(1)}, u32[]{:S(2)}, u32[]{:S(2)}) collective-permute-start(bf16[768,64]{1,0:T(8,128)(2,1)S(1)} %pad_maximum_fusion.refs_2_), channel_id=1, source_target_pairs={{0,4},{1,5},{2,6},{3,7},{4,0},{5,1},{6,2},{7,3},{8,12},{9,13},{10,... | collective-permute-start | bytes 294920 | tf_op jit(solution)/shard_map/ppermute | solution.py:358
  225.4 17.5 %collective-permute-start.25 = (bf16[768,64]{1,0:T(8,128)(2,1)S(1)}, bf16[768,64]{1,0:T(8,128)(2,1)S(1)}, u32[]{:S(2)}, u32[]{:S(2)}) collective-permute-start(bf16[768,64]{1,0:T(8,128)(2,1)S(1)} %pad_maximum_fusion.refs_2_), channel_id=1, source_target_pairs={{0,8},{1,9},{2,10},{3,11},{4,12},{5,13},{6,14},{7,15},{8,0},{9,1},... | collective-permute-start | bytes 294920 | tf_op jit(solution)/shard_map/ppermute | solution.py:358
  228.8 14.2 %collective-permute-start.26 = (bf16[768,64]{1,0:T(8,128)(2,1)S(1)}, bf16[768,64]{1,0:T(8,128)(2,1)S(1)}, u32[]{:S(2)}, u32[]{:S(2)}) collective-permute-start(bf16[768,64]{1,0:T(8,128)(2,1)S(1)} %pad_maximum_fusion.refs_2_), channel_id=1, source_target_pairs={{0,12},{1,13},{2,14},{3,15},{4,8},{5,9},{6,10},{7,11},{8,4},{9,5},... | collective-permute-start | bytes 294920 | tf_op jit(solution)/shard_map/ppermute | solution.py:358
  229.1 13.9 %copy-start.8 = (bf16[16,64,1792]{2,1,0:T(8,128)(2,1)S(1)}, bf16[16,64,1792]{2,1,0:T(8,128)(2,1)}, u32[]{:S(2)}) copy-start(bf16[16,64,1792]{2,1,0:T(8,128)(2,1)} %refs_6_.11) | copy-start | bytes 11010052
  229.1 13.9 %copy-start.14 = (s32[65]{0:T(128)S(1)}, s32[65]{0:T(128)}, u32[]{:S(2)}) copy-start(s32[65]{0:T(128)} %pad_add_fusion.1.refs_0_) | copy-start | bytes 784
  229.1 24.0 %copy-start.1 = (s32[16]{0:T(128)S(1)}, s32[16]{0:T(128)}, u32[]{:S(2)}) copy-start(s32[16]{0:T(128)} %param.15) | copy-start | bytes 196
  242.9 2.0 copy-start.2
  (4 other events, 3.7 us)

commit v3 on v2

--- a/solution.py
+++ b/solution.py
@@ -7,8 +7,10 @@
 
 lowrank_scale = 2.0
 TILE = 256
-KEPT = 3
-VMEM_LIMIT = 30 * 1024 * 1024
+KEPT = 4
+PIECE = 512
+MIDDLE = 0.0
+VMEM_LIMIT = 23 * 1024 * 1024
 
 
 def chip_at(place, chips):
@@ -26,7 +28,7 @@
     return pairs
 
 
-def pass_call(meta, first, blocks, down, gate_matrix, up_matrix, kept, earlier, tiles, block_len, want_reduced):
+def pass_call(meta, first, blocks, down, gate_matrix, up_matrix, kept, earlier, tiles, block_len, want_reduced, threaded=(), share=0.0):
     width, columns = gate_matrix.shape
     rank = down.shape[0]
     fresh = kept is None
@@ -58,8 +60,9 @@
             prod_ref, act_ref, kept_gate, kept_up = rest[:4]
             rest = rest[4:]
         else:
-            prod_ref, act_ref, kept_gate, kept_up = rest[4:8]
-            rest = rest[8:]
+            rest = rest[4 + len(threaded):]
+            prod_ref, act_ref, kept_gate, kept_up = rest[:4]
+            rest = rest[4 + len(threaded):]
         if want_reduced:
             reduced_ref = rest[0]
             rest = rest[1:]
@@ -121,15 +124,18 @@
                         out_sem.at[slot, 2 * b + n]))
             return made
 
-        def compute(done, tile_at, gate_tile, up_tile):
+        def compute(done, tile_at, gate_tiles, up_tiles, which):
             @pl.when(done >= 2)
             def _():
                 wait(out_copies(done - 2, tile_at))
 
             slot = lax.rem(done, 2)
-            rows_in = held[...]
-            gate_out = jnp.dot(rows_in, gate_tile, preferred_element_type=jnp.float32)
-            up_out = jnp.dot(rows_in, up_tile, preferred_element_type=jnp.float32)
+            gate_out = jnp.zeros((rows, TILE), jnp.float32)
+            up_out = gate_out
+            for k in range(0, width, PIECE):
+                rows_in = held[:, k:k + PIECE]
+                gate_out += jnp.dot(rows_in, gate_tiles[which, k:k + PIECE, :], preferred_element_type=jnp.float32)
+                up_out += jnp.dot(rows_in, up_tiles[which, k:k + PIECE, :], preferred_element_type=jnp.float32)
             for b in range(count):
                 at = slice(b * block_len, (b + 1) * block_len)
                 gate_part = gate_out[at]
@@ -143,7 +149,7 @@
             def on_kept(t, carry):
                 if fresh:
                     wait(kept_copies(t))
-                compute(t, t, kept_gate[t], kept_up[t])
+                compute(t, t, kept_gate, kept_up, t)
                 return carry
 
             lax.fori_loop(0, n_kept, on_kept, 0)
@@ -151,7 +157,7 @@
             def on_streamed(s, carry):
                 wait(stream_copies(s))
                 slot = lax.rem(s, 2)
-                compute(n_kept + s, first_streamed + s, gate_in[slot], up_in[slot])
+                compute(n_kept + s, first_streamed + s, gate_in, up_in, slot)
 
                 @pl.when(s + 2 < n_streamed)
                 def _():
@@ -178,8 +184,11 @@
     aliases = {}
     if not fresh:
         in_specs += [any_spec, any_spec, vmem_spec, vmem_spec]
-        aliases = {len(operands) + k: k for k in range(4)}
-        operands += list(earlier) + list(kept)
+        in_specs += [any_spec] * len(threaded)
+        aliases = {len(operands) + k: k for k in range(4 + len(threaded))}
+        operands += list(earlier) + list(kept) + list(threaded)
+        out_specs += [any_spec] * len(threaded)
+        out_shape += [jax.ShapeDtypeStruct(v.shape, v.dtype) for v in threaded]
     if want_reduced:
         out_specs.append(vmem_spec)
         out_shape.append(jax.ShapeDtypeStruct((rows, rank), jnp.bfloat16))
@@ -208,9 +217,25 @@
         input_output_aliases=aliases,
         compiler_params=pltpu.CompilerParams(dimension_semantics=("arbitrary",), vmem_limit_bytes=VMEM_LIMIT),
         cost_estimate=pl.CostEstimate(
-            flops=4 * rows * width * TILE * len(tiles),
-            bytes_accessed=4 * width * TILE * (len(tiles) if fresh else n_streamed), transcendentals=0),
+            flops=int(share * 4 * rows * width * TILE * len(tiles)), bytes_accessed=1024 + int(share * 4 * width * TILE * len(tiles)), transcendentals=0),
     )(*operands)
+
+
+def after_call(values, other):
+    any_spec = pl.BlockSpec(memory_space=pl.ANY)
+
+    def kernel(*refs):
+        pass
+
+    return pl.pallas_call(
+        kernel,
+        in_specs=[any_spec] * (len(values) + 1),
+        out_specs=[any_spec] * len(values),
+        out_shape=[jax.ShapeDtypeStruct(v.shape, v.dtype) for v in values],
+        input_output_aliases={k: k for k in range(len(values))},
+        compiler_params=pltpu.CompilerParams(vmem_limit_bytes=1024 * 1024),
+        cost_estimate=pl.CostEstimate(flops=0, bytes_accessed=0, transcendentals=0),
+    )(*values, other)
 
 
 def place_call(meta, owned, row_total, block_len):
@@ -375,30 +400,38 @@
         kept = out[2:4]
         owned.append(out[-1])
         first += len(blocks)
+        from_left, from_right = after_call((from_left, from_right), out[-1])
         blocks = [[(v, False, 0), (flip(v, 1), True, 0)] for v in (from_left, from_right)]
     cut = rows_here // 2
     last_low = send(from_left[:cut], right)
     last_high = send(from_right[cut:], left)
     early = place_call(meta, owned, row_total, block_len)
-    for bits in (1, 2, 4, 8):
-        early = early + flip(early, bits)
-    *state, kept_gate, kept_up, part = pass_call(
-        meta, first, blocks, down, *weights, kept, state, all_tiles, block_len, True)
-    kept = (kept_gate, kept_up)
+    early = early + flip(early, 1)
+    met = flip(early, 2)
+    *state, kept_gate, kept_up, early, part = pass_call(
+        meta, first, blocks, down, *weights, kept, state, all_tiles[:KEPT], block_len, True, (early,))
+    early = early + met
+    met = flip(early, 4)
+    *state, kept_gate, kept_up, early, part = pass_call(
+        meta, first, blocks, down, *weights, (kept_gate, kept_up), state, all_tiles[KEPT:], block_len, False, (early, part), MIDDLE)
+    early = early + met
+    met = flip(early, 8)
     first += 2
+    last_low, last_high = after_call((last_low, last_high), part)
     pieces = [
         (last_low, False, 0), (flip(last_low, 1), True, 0),
         (last_high, False, cut), (flip(last_high, 1), True, cut),
     ]
     mine = late_call(meta, first, pieces, down, part, block_len)
-    on_chip = mine + flip(mine, 1)
-    across = flip(mine, 2) + flip(mine, 3)
-    both = jnp.concatenate([on_chip, across], axis=0)
-    late = [both] + [flip(both, 4 * k) for k in range(1, chips // 2)]
-    for tiles in (all_tiles[KEPT:], all_tiles[:KEPT]):
-        out = pass_call(meta, first, [pieces], down, *weights, kept, state, tiles, block_len, False)
-        state, kept = out[:2], out[2:]
-    return finish_call(meta, last_at, early, late, lowrank_up, *state, block_len)
+    near = [flip(mine, bits) for bits in (1, 2, 3)]
+    *state, kept_gate, kept_up, early, mine = pass_call(
+        meta, first, [pieces], down, *weights, (kept_gate, kept_up), state, all_tiles[:KEPT], block_len, False, (early, mine), 1.0)
+    early = early + met
+    both = jnp.concatenate([mine + near[0], near[1] + near[2]], axis=0)
+    far = [flip(both, 4 * k) for k in range(1, chips // 2)]
+    *state, kept_gate, kept_up, both = pass_call(
+        meta, first, [pieces], down, *weights, (kept_gate, kept_up), state, all_tiles[KEPT:], block_len, False, (both,), 1.0)
+    return finish_call(meta, last_at, early, [both] + far, lowrank_up, *state, block_len)
 
 
 def on_device(

time: 256 us -> 243 us (0.949)
  waiting for transfers between devices: 58.1 us -> 45.6 us
  Pallas kernels: 159 us -> 149 us
  local copies, waits for them, and re-layouts: 11.3 us -> 16.1 us
  other arithmetic: 2.47 us -> 6.2 us
    ppermute x8, waiting for transfers between devices: 19.1 us -> 0.02 us  [send(): return lax.ppermute(value, 'tensor', pairs)]
    pallas_call x6 -> x7, Pallas kernels: 149 us -> 139 us  [pass_call(): pl.pallas_call(kernel, grid_spec=pltpu.PrefetchScalarGridSpec(num_scalar_...]
    ppermute x19, waiting for transfers between devices: 39 us -> 45.6 us  [flip(): lax.ppermute(value, 'tensor', [(d, d ^ bits) for d in range(2 * chips)])]
    unnamed x50 -> x78, local copies, waits for them, and re-layouts: 7.61 us -> 12.4 us
    add x6, other arithmetic: 0.35 us -> 4.08 us  [the longest x3 3.06 us: on_ring(): early = early + met]
  transfers between devices with their start and end apart: 27 -> 27, of which waited for: 5 -> 12; matrix products, arithmetic and copies ran while one was open for 2% -> 4% of each run, Pallas kernels for 59% -> 50%
where the time goes in v3:
time: 243 us; the launch traced here: 239 us
  Pallas kernels  149 us (61%)
  waiting for transfers between devices  45.6 us (19%)
  starting transfers between devices  22 us (9%)
  local copies, waits for them, and re-layouts  16.1 us (7%)
  other arithmetic  6.2 us (3%)
    pallas_call x7, Pallas kernels, pass_call(): pl.pallas_call(kernel, grid_spec=pltpu.PrefetchScalarGridSpec(num_scalar_...  139 us
    ppermute x19, waiting for transfers between devices, flip(): lax.ppermute(value, 'tensor', [(d, d ^ bits) for d in range(2 * chips)])  45.6 us
    ppermute x19, starting transfers between devices, flip(): lax.ppermute(value, 'tensor', [(d, d ^ bits) for d in range(2 * chips)])  13.8 us
    unnamed x78, local copies, waits for them, and re-layouts  12.4 us
    ppermute x8, starting transfers between devices, send(): return lax.ppermute(value, 'tensor', pairs)  8.21 us
    pallas_call x1, Pallas kernels, finish_call(): pl.pallas_call(kernel, grid_spec=pltpu.PrefetchScalarGridSpec(num_scalar_...  8.11 us
  transfers between devices with their start and end apart: 27, of which 12 were waited for; matrix products, arithmetic and copies ran while one was open for 4% of the time, Pallas kernels for 50%

profile of v3, /device:TPU:4, one launch (start us, length us, event | category | flops | bytes accessed | tf_op | source)
XLA Modules:
  0.0 239.3 jit_solution(18040075379154149374)
XLA Ops:
  0.0 1.6 collective-permute-start
  2.1 0.7 compare_select_fusion.1
  2.8 1.3 gather_fusion
  4.1 0.7 compare_select_fusion
  6.3 0.7 stack.30
  7.8 1.0 copy-done.34
  8.8 28.8 %shard_map.91 = (bf16[1024,1792]{1,0:T(8,128)(2,1)}, bf16[1024,1792]{1,0:T(8,128)(2,1)}, bf16[4,8192,256]{2,1,0:T(8,128)(2,1)S(1)}, bf16[4,8192,256]{2,1,0:T(8,128)(2,1)S(1)}, bf16[128,64]{1,0:T(8,128)(2,1)}) custom-call(s32[65]{0:T(128)} %pad_add_fusion.1.refs_0_, bf16[64,8192]{1,0:T(8,128)(2,1)} %refs_1_.1, bf16[64,8192]{1,0:T(8,128)(2,1)} %copy-done.34, ...), custom_call_target="tpu_custom_call" | custom-call | bytes 1024 | tf_op jit(solution)/shard_map/pallas_call | solution.py:197
  37.6 0.7 copy-done.24
  38.9 1.6 collective-permute-start.3
  41.0 1.5 collective-permute-done.6.refs_4_
  42.5 1.0 copy-done.37
  43.6 28.3 %shard_map.93 = (bf16[1024,1792]{1,0:T(8,128)(2,1)}, bf16[1024,1792]{1,0:T(8,128)(2,1)}, bf16[4,8192,256]{2,1,0:T(8,128)(2,1)S(1)}, bf16[4,8192,256]{2,1,0:T(8,128)(2,1)S(1)}, bf16[256,64]{1,0:T(8,128)(2,1)}) custom-call(s32[65]{0:T(128)} %pad_add_fusion.1.refs_0_, ...), custom_call_target="tpu_custom_call", output_to_operand_aliasing={{0}: (8, {}), {1}: (9, {}), {2}: (10, {}), {3}: (11, {})} | custom-call | bytes 1024 | tf_op jit(solution)/shard_map/pallas_call | solution.py:197
  71.9 0.8 copy-done.20
  73.2 1.6 collective-permute-start.7
  75.4 1.5 collective-permute-done.9.refs_2_
  76.9 1.0 copy-done.38
  77.9 28.4 %shard_map.95 = (bf16[1024,1792]{1,0:T(8,128)(2,1)}, bf16[1024,1792]{1,0:T(8,128)(2,1)}, bf16[4,8192,256]{2,1,0:T(8,128)(2,1)S(1)}, bf16[4,8192,256]{2,1,0:T(8,128)(2,1)S(1)}, bf16[256,64]{1,0:T(8,128)(2,1)}) custom-call(s32[65]{0:T(128)} %pad_add_fusion.1.refs_0_, ...), custom_call_target="tpu_custom_call", output_to_operand_aliasing={{0}: (8, {}), {1}: (9, {}), {2}: (10, {}), {3}: (11, {})} | custom-call | bytes 1024 | tf_op jit(solution)/shard_map/pallas_call | solution.py:197
  106.3 0.8 copy-done.22
  107.7 1.6 collective-permute-start.11
  109.8 0.8 copy-done.23
  111.3 1.5 collective-permute-done.15
  112.9 1.5 collective-permute-start.16
  114.5 12.9 %collective-permute-done.16 = bf16[1024,64]{1,0:T(8,128)(2,1)S(1)} collective-permute-done((bf16[1024,64]{1,0:T(8,128)(2,1)S(1)}, bf16[1024,64]{1,0:T(8,128)(2,1)S(1)}, u32[]{:S(2)}, u32[]{:S(2)}) %collective-permute-start.16) | collective-permute-done | bytes 131104 | tf_op jit(solution)/shard_map/ppermute | solution.py:383
  127.4 0.9 copy-done.29
  128.8 16.3 %shard_map.98 = (bf16[1024,1792]{1,0:T(8,128)(2,1)}, bf16[1024,1792]{1,0:T(8,128)(2,1)}, bf16[4,8192,256]{2,1,0:T(8,128)(2,1)S(1)}, bf16[4,8192,256]{2,1,0:T(8,1...) custom-call(s32[65]{0:T(128)} %pad_add_fusion.1.refs_0_, ...), custom_call_target="tpu_custom_call", output_to_operand_aliasing={{0}: (8, {}), {1}: (9, {}), {2}: (10, {}), {3}: (11, {}), {... | custom-call | bytes 1024 | tf_op jit(solution)/shard_map/pallas_call | solution.py:197
  145.1 1.0 add.168.refs_11_
  146.2 7.5 %collective-permute-done.19 = bf16[1024,64]{1,0:T(8,128)(2,1)S(1)} collective-permute-done((bf16[1024,64]{1,0:T(8,128)(2,1)S(1)}, bf16[1024,64]{1,0:T(8,128)(2,1)S(1)}, u32[]{:S(2)}, u32[]{:S(2)}) %collective-permute-start.19) | collective-permute-done | bytes 131104 | tf_op jit(solution)/shard_map/ppermute | solution.py:383
  153.7 15.8 %shard_map.99 = (bf16[1024,1792]{1,0:T(8,128)(2,1)}, bf16[1024,1792]{1,0:T(8,128)(2,1)}, bf16[4,8192,256]{2,1,0:T(8,128)(2,1)S(1)}, bf16[4,8192,256]{2,1,0:T(8,1...) custom-call(s32[65]{0:T(128)} %pad_add_fusion.1.refs_0_, ...), custom_call_target="tpu_custom_call", output_to_operand_aliasing={{0}: (7, {}), {1}: (8, {}), {2}: (9, {}), {3}: (10, {}), {4... | custom-call | bytes 1024 | tf_op jit(solution)/shard_map/pallas_call | solution.py:197
  169.6 0.8 copy-done.18
  170.9 1.0 add.169.refs_11_
  171.9 3.4 %collective-permute-start.20 = (bf16[1024,64]{1,0:T(8,128)(2,1)S(1)}, bf16[1024,64]{1,0:T(8,128)(2,1)S(1)}, u32[]{:S(2)}, u32[]{:S(2)}) collective-permute-start(bf16[1024,64]{1,0:T(8,128)(2,1)S(1)} %add.169.refs_11_), channel_id=1, source_target_pairs={{0,8},{1,9},{2,10},{3,11},{4,12},{5,13},{6,14},{7,15},{8,0},{9,1},... | collective-permute-start | bytes 393224 | tf_op jit(solution)/shard_map/ppermute | solution.py:383
  175.4 0.9 copy-done.19
  176.3 1.4 shard_map.101.refs_12_
  177.7 0.7 collective-permute-start.22
  178.9 1.0 collective-permute-start.21
  179.9 3.5 %collective-permute-done.22 = bf16[384,64]{1,0:T(8,128)(2,1)S(1)} collective-permute-done((bf16[384,64]{1,0:T(8,128)(2,1)S(1)}, bf16[384,64]{1,0:T(8,128)(2,1)S(1)}, u32[]{:S(2)}, u32[]{:S(2)}) %collective-permute-start.22) | collective-permute-done | bytes 49184 | tf_op jit(solution)/shard_map/ppermute | solution.py:383
  183.5 3.9 %collective-permute-done.20 = bf16[1024,64]{1,0:T(8,128)(2,1)S(1)} collective-permute-done((bf16[1024,64]{1,0:T(8,128)(2,1)S(1)}, bf16[1024,64]{1,0:T(8,128)(2,1)S(1)}, u32[]{:S(2)}, u32[]{:S(2)}) %collective-permute-start.20) | collective-permute-done | bytes 131104 | tf_op jit(solution)/shard_map/ppermute | solution.py:383
  187.5 8.2 %shard_map.102 = (bf16[1024,1792]{1,0:T(8,128)(2,1)}, bf16[1024,1792]{1,0:T(8,128)(2,1)}, bf16[4,8192,256]{2,1,0:T(8,128)(2,1)S(1)}, bf16[4,8192,256]{2,1,0:T(8,...) custom-call(s32[65]{0:T(128)} %pad_add_fusion.1.refs_0_, ...), custom_call_target="tpu_custom_call", output_to_operand_aliasing={{0}: (7, {}), {1}: (8, {}), {2}: (9, {}), {3}: (10, {}), {4... | custom-call | flops 4294967296 | bytes 33555456 | tf_op jit(solution)/shard_map/pallas_call | solution.py:197
  195.7 0.9 add.171
  196.7 0.8 collective-permute-start.24
  197.5 3.4 %collective-permute-start.25 = (bf16[768,64]{1,0:T(8,128)(2,1)S(1)}, bf16[768,64]{1,0:T(8,128)(2,1)S(1)}, u32[]{:S(2)}, u32[]{:S(2)}) collective-permute-start(bf16[768,64]{1,0:T(8,128)(2,1)S(1)} %pad_maximum_fusion.refs_11_), channel_id=1, source_target_pairs={{0,8},{1,9},{2,10},{3,11},{4,12},{5,13},{6,14},{7,15},{8,0},{9,1},... | collective-permute-start | bytes 294920 | tf_op jit(solution)/shard_map/ppermute | solution.py:383
  201.1 1.0 add.170.refs_1_
  202.2 4.6 %collective-permute-done.24.refs_3_ = bf16[768,64]{1,0:T(8,128)(2,1)S(1)} collective-permute-done((bf16[768,64]{1,0:T(8,128)(2,1)S(1)}, bf16[768,64]{1,0:T(8,128)(2,1)S(1)}, u32[]{:S(2)}, u32[]{:S(2)}) %collective-permute-start.24) | collective-permute-done | bytes 98336 | tf_op jit(solution)/shard_map/ppermute | solution.py:383
  206.7 8.3 %collective-permute-done.25.refs_4_ = bf16[768,64]{1,0:T(8,128)(2,1)S(1)} collective-permute-done((bf16[768,64]{1,0:T(8,128)(2,1)S(1)}, bf16[768,64]{1,0:T(8,128)(2,1)S(1)}, u32[]{:S(2)}, u32[]{:S(2)}) %collective-permute-start.25) | collective-permute-done | bytes 98336 | tf_op jit(solution)/shard_map/ppermute | solution.py:383
  215.1 13.0 %shard_map.103 = (bf16[1024,1792]{1,0:T(8,128)(2,1)}, bf16[1024,1792]{1,0:T(8,128)(2,1)}, bf16[4,8192,256]{2,1,0:T(8,128)(2,1)S(1)}, bf16[4,8192,256]{2,1,0:T(8,128)(2,1)S(1)}, bf16[768,64]{1,0:T(8,128)(2,1)}) custom-call(s32[65]{0:T(128)} %pad_add_fusion.1.refs_0_, ...), custom_call_target="tpu_custom_call", output_to_operand_aliasing={{0}: (7, {}), {1}: (8, {}), {2}: (9, {}), {3}: (10, {}), {4... | custom-call | flops 3221225472 | bytes 25166848 | tf_op jit(solution)/shard_map/pallas_call | solution.py:197
  228.2 2.0 copy-done.2
  230.2 0.9 copy-done.16
  231.2 8.1 %shard_map.104 = bf16[1024,1792]{1,0:T(8,128)(2,1)} custom-call(s32[65]{0:T(128)S(1)} %copy-done.28, bf16[1024,64]{1,0:T(8,128)(2,1)S(1)} %add.170.refs_1_, bf16[768,64]{1,0:T(8,128)(2,1)S(1)} %copy-done.16, bf16[768,64]{1,0:T(8,128)(2,1)S(1)} %collective-permute-done.24.refs_3_, ...), custom_call_target="tpu_custom_call", output_to_operand_aliasing={{}: (7, {})} | custom-call | flops 939524096 | bytes 11010048 | tf_op jit(solution)/shard_map/pallas_call | solution.py:328
  (124 shorter events, 8.8 us)
Async XLA Ops:
  0.0 4.7 %copy-start = (s32[16]{0:T(128)S(1)}, s32[16]{0:T(128)}, u32[]{:S(2)}) copy-start(s32[16]{0:T(128)} %param.15) | copy-start | bytes 196
  0.0 7.8 %collective-permute-start.2 = (bf16[64,8192]{1,0:T(8,128)(2,1)}, bf16[64,8192]{1,0:T(8,128)(2,1)S(1)}, u32[]{:S(2)}, u32[]{:S(2)}) collective-permute-start(bf16[64,8192]{1,0:T(8,128)(2,1)} %refs_1_.1), channel_id=1, source_target_pairs={{0,1},{1,0},{2,3},{3,2},{4,5},{5,4},{6,7},{7,6},{8,9},{9,8},{10,11... | collective-permute-start | bytes 3145736 | tf_op jit(solution)/shard_map/ppermute | solution.py:383
  0.0 37.6 %collective-permute-start = (bf16[64,8192]{1,0:T(8,128)(2,1)}, bf16[64,8192]{1,0:T(8,128)(2,1)S(1)}, u32[]{:S(2)}, u32[]{:S(2)}) collective-permute-start(bf16[64,8192]{1,0:T(8,128)(2,1)} %refs_1_.1), channel_id=1, source_target_pairs={{0,4},{1,5},{4,8},{5,9},{8,12},{9,13},{12,14},{13,15},{14,10},{15,... | collective-permute-start | bytes 3145736 | tf_op jit(solution)/shard_map/ppermute | solution.py:380
  1.6 35.9 %collective-permute-start.1 = (bf16[64,8192]{1,0:T(8,128)(2,1)}, bf16[64,8192]{1,0:T(8,128)(2,1)S(1)}, u32[]{:S(2)}, u32[]{:S(2)}) collective-permute-start(bf16[64,8192]{1,0:T(8,128)(2,1)} %refs_1_.1), channel_id=1, source_target_pairs={{0,2},{1,3},{4,0},{5,1},{8,4},{9,5},{12,8},{13,9},{14,12},{15,13},... | collective-permute-start | bytes 3145736 | tf_op jit(solution)/shard_map/ppermute | solution.py:380
  38.4 4.2 %copy-start.11 = (bf16[64,8192]{1,0:T(8,128)(2,1)}, bf16[64,8192]{1,0:T(8,128)(2,1)S(1)}, u32[]{:S(2)}) copy-start(bf16[64,8192]{1,0:T(8,128)(2,1)S(1)} %get-tuple-element.51.refs_3_) | copy-start | bytes 3145732
  38.4 2.7 %collective-permute-start.5 = (bf16[64,8192]{1,0:T(8,128)(2,1)S(1)}, bf16[64,8192]{1,0:T(8,128)(2,1)S(1)}, u32[]{:S(2)}, u32[]{:S(2)}) collective-permute-start(bf16[64,8192]{1,0:T(8,128)(2,1)S(1)} %get-tuple-element.50.refs_1_), channel_id=1, source_target_pairs={{0,1},{1,0},{2,3},{3,2},{4,5},{5,4},{6,7},{7,6},{8,9},{9,8},{10,11... | collective-permute-start | bytes 3145736 | tf_op jit(solution)/shard_map/ppermute | solution.py:383
  38.4 4.2 %collective-permute-start.6 = (bf16[64,8192]{1,0:T(8,128)(2,1)S(1)}, bf16[64,8192]{1,0:T(8,128)(2,1)S(1)}, u32[]{:S(2)}, u32[]{:S(2)}) collective-permute-start(bf16[64,8192]{1,0:T(8,128)(2,1)S(1)} %get-tuple-element.51.refs_3_), channel_id=1, source_target_pairs={{0,1},{1,0},{2,3},{3,2},{4,5},{5,4},{6,7},{7,6},{8,9},{9,8},{10,11... | collective-permute-start | bytes 3145736 | tf_op jit(solution)/shard_map/ppermute | solution.py:383
  38.9 33.0 %collective-permute-start.3 = (bf16[64,8192]{1,0:T(8,128)(2,1)S(1)}, bf16[64,8192]{1,0:T(8,128)(2,1)S(1)}, u32[]{:S(2)}, u32[]{:S(2)}) collective-permute-start(bf16[64,8192]{1,0:T(8,128)(2,1)S(1)} %get-tuple-element.50.refs_1_), channel_id=1, source_target_pairs={{0,4},{1,5},{4,8},{5,9},{8,12},{9,13},{12,14},{13,15},{14,10},{15,... | collective-permute-start | bytes 3145736 | tf_op jit(solution)/shard_map/ppermute | solution.py:380
  40.5 31.4 %collective-permute-start.4 = (bf16[64,8192]{1,0:T(8,128)(2,1)S(1)}, bf16[64,8192]{1,0:T(8,128)(2,1)S(1)}, u32[]{:S(2)}, u32[]{:S(2)}) collective-permute-start(bf16[64,8192]{1,0:T(8,128)(2,1)S(1)} %get-tuple-element.51.refs_3_), channel_id=1, source_target_pairs={{0,2},{1,3},{4,0},{5,1},{8,4},{9,5},{12,8},{13,9},{14,12},{15,13},... | collective-permute-start | bytes 3145736 | tf_op jit(solution)/shard_map/ppermute | solution.py:380
  72.7 2.7 %collective-permute-start.10 = (bf16[64,8192]{1,0:T(8,128)(2,1)S(1)}, bf16[64,8192]{1,0:T(8,128)(2,1)S(1)}, u32[]{:S(2)}, u32[]{:S(2)}) collective-permute-start(bf16[64,8192]{1,0:T(8,128)(2,1)S(1)} %get-tuple-element.58.refs_3_), channel_id=1, source_target_pairs={{0,1},{1,0},{2,3},{3,2},{4,5},{5,4},{6,7},{7,6},{8,9},{9,8},{10,11... | collective-permute-start | bytes 3145736 | tf_op jit(solution)/shard_map/ppermute | solution.py:383
  72.8 4.0 %collective-permute-start.9 = (bf16[64,8192]{1,0:T(8,128)(2,1)S(1)}, bf16[64,8192]{1,0:T(8,128)(2,1)S(1)}, u32[]{:S(2)}, u32[]{:S(2)}) collective-permute-start(bf16[64,8192]{1,0:T(8,128)(2,1)S(1)} %get-tuple-element.57.refs_1_), channel_id=1, source_target_pairs={{0,1},{1,0},{2,3},{3,2},{4,5},{5,4},{6,7},{7,6},{8,9},{9,8},{10,11... | collective-permute-start | bytes 3145736 | tf_op jit(solution)/shard_map/ppermute | solution.py:383
  73.2 33.0 %collective-permute-start.7 = (bf16[64,8192]{1,0:T(8,128)(2,1)S(1)}, bf16[64,8192]{1,0:T(8,128)(2,1)S(1)}, u32[]{:S(2)}, u32[]{:S(2)}) collective-permute-start(bf16[64,8192]{1,0:T(8,128)(2,1)S(1)} %get-tuple-element.57.refs_1_), channel_id=1, source_target_pairs={{0,4},{1,5},{4,8},{5,9},{8,12},{9,13},{12,14},{13,15},{14,10},{15,... | collective-permute-start | bytes 3145736 | tf_op jit(solution)/shard_map/ppermute | solution.py:380
  74.8 31.5 %collective-permute-start.8 = (bf16[64,8192]{1,0:T(8,128)(2,1)S(1)}, bf16[64,8192]{1,0:T(8,128)(2,1)S(1)}, u32[]{:S(2)}, u32[]{:S(2)}) collective-permute-start(bf16[64,8192]{1,0:T(8,128)(2,1)S(1)} %get-tuple-element.58.refs_3_), channel_id=1, source_target_pairs={{0,2},{1,3},{4,0},{5,1},{8,4},{9,5},{12,8},{13,9},{14,12},{15,13},... | collective-permute-start | bytes 3145736 | tf_op jit(solution)/shard_map/ppermute | solution.py:380
  77.9 31.9 %copy-start.21 = (bf16[256,64]{1,0:T(8,128)(2,1)S(1)}, bf16[256,64]{1,0:T(8,128)(2,1)}, u32[]{:S(2)}) copy-start(bf16[256,64]{1,0:T(8,128)(2,1)} %get-tuple-element.56.refs_2_) | copy-start | bytes 98308
  77.9 31.9 %copy-start.25 = (bf16[128,64]{1,0:T(8,128)(2,1)S(1)}, bf16[128,64]{1,0:T(8,128)(2,1)}, u32[]{:S(2)}) copy-start(bf16[128,64]{1,0:T(8,128)(2,1)} %get-tuple-element.49.refs_2_.refs_1_) | copy-start | bytes 49156
  77.9 31.9 %copy-start.26 = (s32[65]{0:T(128)S(1)}, s32[65]{0:T(128)}, u32[]{:S(2)}) copy-start(s32[65]{0:T(128)} %pad_add_fusion.1.refs_0_) | copy-start | bytes 784
  107.1 20.2 %copy-start.4 = (bf16[64,8192]{1,0:T(8,128)(2,1)}, bf16[64,8192]{1,0:T(8,128)(2,1)S(1)}, u32[]{:S(2)}) copy-start(bf16[64,8192]{1,0:T(8,128)(2,1)S(1)} %get-tuple-element.64.refs_1_) | copy-start | bytes 3145732
  107.1 20.3 %copy-start.5 = (bf16[64,8192]{1,0:T(8,128)(2,1)}, bf16[64,8192]{1,0:T(8,128)(2,1)S(1)}, u32[]{:S(2)}) copy-start(bf16[64,8192]{1,0:T(8,128)(2,1)S(1)} %get-tuple-element.65.refs_3_) | copy-start | bytes 3145732
  107.1 20.2 %collective-permute-start.13 = (bf16[64,8192]{1,0:T(8,128)(2,1)S(1)}, bf16[64,8192]{1,0:T(8,128)(2,1)S(1)}, u32[]{:S(2)}, u32[]{:S(2)}) collective-permute-start(bf16[64,8192]{1,0:T(8,128)(2,1)S(1)} %get-tuple-element.64.refs_1_), channel_id=1, source_target_pairs={{0,1},{1,0},{2,3},{3,2},{4,5},{5,4},{6,7},{7,6},{8,9},{9,8},{10,11... | collective-permute-start | bytes 3145736 | tf_op jit(solution)/shard_map/ppermute | solution.py:383
  107.3 20.1 %collective-permute-start.14 = (bf16[64,8192]{1,0:T(8,128)(2,1)S(1)}, bf16[64,8192]{1,0:T(8,128)(2,1)S(1)}, u32[]{:S(2)}, u32[]{:S(2)}) collective-permute-start(bf16[64,8192]{1,0:T(8,128)(2,1)S(1)} %get-tuple-element.65.refs_3_), channel_id=1, source_target_pairs={{0,1},{1,0},{2,3},{3,2},{4,5},{5,4},{6,7},{7,6},{8,9},{9,8},{10,11... | collective-permute-start | bytes 3145736 | tf_op jit(solution)/shard_map/ppermute | solution.py:383
  107.7 61.8 %collective-permute-start.11 = (bf16[32,8192]{1,0:T(8,128)(2,1)S(1)}, bf16[32,8192]{1,0:T(8,128)(2,1)S(1)}, u32[]{:S(2)}, u32[]{:S(2)}) collective-permute-start(bf16[32,8192]{1,0:T(8,128)(2,1)S(1)} %slice.6), channel_id=1, source_target_pairs={{0,4},{1,5},{4,8},{5,9},{8,12},{9,13},{12,14},{13,15},{14,10},{15,... | collective-permute-start | bytes 1572872 | tf_op jit(solution)/shard_map/ppermute | solution.py:380
  109.4 60.2 %collective-permute-start.12 = (bf16[32,8192]{1,0:T(8,128)(2,1)S(1)}, bf16[32,8192]{1,0:T(8,128)(2,1)S(1)}, u32[]{:S(2)}, u32[]{:S(2)}) collective-permute-start(bf16[32,8192]{1,0:T(8,128)(2,1)S(1)} %slice.7), channel_id=1, source_target_pairs={{0,2},{1,3},{4,0},{5,1},{8,4},{9,5},{12,8},{13,9},{14,12},{15,13},... | collective-permute-start | bytes 1572872 | tf_op jit(solution)/shard_map/ppermute | solution.py:380
  111.3 1.6 collective-permute-start.15
  112.9 14.5 %copy-start.32 = (bf16[1024,64]{1,0:T(8,128)(2,1)}, bf16[1024,64]{1,0:T(8,128)(2,1)S(1)}, u32[]{:S(2)}) copy-start(bf16[1024,64]{1,0:T(8,128)(2,1)S(1)} %add.167.refs_12_) | copy-start | bytes 393220
  112.9 14.4 %collective-permute-start.16 = (bf16[1024,64]{1,0:T(8,128)(2,1)S(1)}, bf16[1024,64]{1,0:T(8,128)(2,1)S(1)}, u32[]{:S(2)}, u32[]{:S(2)}) collective-permute-start(bf16[1024,64]{1,0:T(8,128)(2,1)S(1)} %add.167.refs_12_), channel_id=1, source_target_pairs={{0,2},{1,3},{2,0},{3,1},{4,6},{5,7},{6,4},{7,5},{8,10},{9,11},{10,... | collective-permute-start | bytes 393224 | tf_op jit(solution)/shard_map/ppermute | solution.py:383
  146.1 7.6 %copy-start.33 = (bf16[1024,64]{1,0:T(8,128)(2,1)}, bf16[1024,64]{1,0:T(8,128)(2,1)S(1)}, u32[]{:S(2)}) copy-start(bf16[1024,64]{1,0:T(8,128)(2,1)S(1)} %add.168.refs_11_) | copy-start | bytes 393220
  146.1 7.6 %collective-permute-start.19 = (bf16[1024,64]{1,0:T(8,128)(2,1)S(1)}, bf16[1024,64]{1,0:T(8,128)(2,1)S(1)}, u32[]{:S(2)}, u32[]{:S(2)}) collective-permute-start(bf16[1024,64]{1,0:T(8,128)(2,1)S(1)} %add.168.refs_11_), channel_id=1, source_target_pairs={{0,4},{1,5},{2,6},{3,7},{4,0},{5,1},{6,2},{7,3},{8,12},{9,13},{10,... | collective-permute-start | bytes 393224 | tf_op jit(solution)/shard_map/ppermute | solution.py:383
  153.7 21.6 %copy-start.3 = (bf16[1,64,8192]{2,1,0:T(8,128)(2,1)S(1)}, bf16[1,64,8192]{2,1,0:T(8,128)(2,1)}, u32[]{:S(2)}) copy-start(bf16[1,64,8192]{2,1,0:T(8,128)(2,1)} %param.12) | copy-start | bytes 3145732
  153.7 21.6 %copy-start.27 = (s32[65]{0:T(128)S(1)}, s32[65]{0:T(128)}, u32[]{:S(2)}) copy-start(s32[65]{0:T(128)} %pad_add_fusion.1.refs_0_) | copy-start | bytes 784
  170.4 17.1 %copy-start.6 = (bf16[32,8192]{1,0:T(8,128)(2,1)}, bf16[32,8192]{1,0:T(8,128)(2,1)S(1)}, u32[]{:S(2)}) copy-start(bf16[32,8192]{1,0:T(8,128)(2,1)S(1)} %get-tuple-element.77.refs_1_) | copy-start | bytes 1572868
  170.4 17.1 %copy-start.7 = (bf16[32,8192]{1,0:T(8,128)(2,1)}, bf16[32,8192]{1,0:T(8,128)(2,1)S(1)}, u32[]{:S(2)}) copy-start(bf16[32,8192]{1,0:T(8,128)(2,1)S(1)} %get-tuple-element.78.refs_3_) | copy-start | bytes 1572868
  170.4 4.9 %collective-permute-start.17 = (bf16[32,8192]{1,0:T(8,128)(2,1)S(1)}, bf16[32,8192]{1,0:T(8,128)(2,1)S(1)}, u32[]{:S(2)}, u32[]{:S(2)}) collective-permute-start(bf16[32,8192]{1,0:T(8,128)(2,1)S(1)} %get-tuple-element.77.refs_1_), channel_id=1, source_target_pairs={{0,1},{1,0},{2,3},{3,2},{4,5},{5,4},{6,7},{7,6},{8,9},{9,8},{10,11... | collective-permute-start | bytes 1572872 | tf_op jit(solution)/shard_map/ppermute | solution.py:383
  170.4 4.9 %collective-permute-start.18 = (bf16[32,8192]{1,0:T(8,128)(2,1)S(1)}, bf16[32,8192]{1,0:T(8,128)(2,1)S(1)}, u32[]{:S(2)}, u32[]{:S(2)}) collective-permute-start(bf16[32,8192]{1,0:T(8,128)(2,1)S(1)} %get-tuple-element.78.refs_3_), channel_id=1, source_target_pairs={{0,1},{1,0},{2,3},{3,2},{4,5},{5,4},{6,7},{7,6},{8,9},{9,8},{10,11... | collective-permute-start | bytes 1572872 | tf_op jit(solution)/shard_map/ppermute | solution.py:383
  171.9 15.6 %copy-start.31 = (bf16[1024,64]{1,0:T(8,128)(2,1)}, bf16[1024,64]{1,0:T(8,128)(2,1)S(1)}, u32[]{:S(2)}) copy-start(bf16[1024,64]{1,0:T(8,128)(2,1)S(1)} %add.169.refs_11_) | copy-start | bytes 393220
  171.9 15.5 %collective-permute-start.20 = (bf16[1024,64]{1,0:T(8,128)(2,1)S(1)}, bf16[1024,64]{1,0:T(8,128)(2,1)S(1)}, u32[]{:S(2)}, u32[]{:S(2)}) collective-permute-start(bf16[1024,64]{1,0:T(8,128)(2,1)S(1)} %add.169.refs_11_), channel_id=1, source_target_pairs={{0,8},{1,9},{2,10},{3,11},{4,12},{5,13},{6,14},{7,15},{8,0},{9,1},... | collective-permute-start | bytes 393224 | tf_op jit(solution)/shard_map/ppermute | solution.py:383
  175.3 12.2 %copy-start.8 = (bf16[32,8192]{1,0:T(8,128)(2,1)}, bf16[32,8192]{1,0:T(8,128)(2,1)S(1)}, u32[]{:S(2)}) copy-start(bf16[32,8192]{1,0:T(8,128)(2,1)S(1)} %collective-permute-done.17.refs_2_) | copy-start | bytes 1572868
  176.3 11.2 %copy-start.9 = (bf16[32,8192]{1,0:T(8,128)(2,1)}, bf16[32,8192]{1,0:T(8,128)(2,1)S(1)}, u32[]{:S(2)}) copy-start(bf16[32,8192]{1,0:T(8,128)(2,1)S(1)} %collective-permute-done.18.refs_4_) | copy-start | bytes 1572868
  177.7 9.8 %copy-start.17 = (bf16[384,64]{1,0:T(8,128)(2,1)}, bf16[384,64]{1,0:T(8,128)(2,1)S(1)}, u32[]{:S(2)}) copy-start(bf16[384,64]{1,0:T(8,128)(2,1)S(1)} %shard_map.101.refs_12_) | copy-start | bytes 147460
  177.7 5.7 %collective-permute-start.22 = (bf16[384,64]{1,0:T(8,128)(2,1)S(1)}, bf16[384,64]{1,0:T(8,128)(2,1)S(1)}, u32[]{:S(2)}, u32[]{:S(2)}) collective-permute-start(bf16[384,64]{1,0:T(8,128)(2,1)S(1)} %shard_map.101.refs_12_), channel_id=1, source_target_pairs={{0,2},{1,3},{2,0},{3,1},{4,6},{5,7},{6,4},{7,5},{8,10},{9,11},{10,... | collective-permute-start | bytes 147464 | tf_op jit(solution)/shard_map/ppermute | solution.py:383
  178.4 5.1 %collective-permute-start.23 = (bf16[384,64]{1,0:T(8,128)(2,1)S(1)}, bf16[384,64]{1,0:T(8,128)(2,1)S(1)}, u32[]{:S(2)}, u32[]{:S(2)}) collective-permute-start(bf16[384,64]{1,0:T(8,128)(2,1)S(1)} %shard_map.101.refs_12_), channel_id=1, source_target_pairs={{0,3},{1,2},{2,1},{3,0},{4,7},{5,6},{6,5},{7,4},{8,11},{9,10},{10,... | collective-permute-start | bytes 147464 | tf_op jit(solution)/shard_map/ppermute | solution.py:383
  178.9 8.5 %collective-permute-start.21 = (bf16[384,64]{1,0:T(8,128)(2,1)S(1)}, bf16[384,64]{1,0:T(8,128)(2,1)S(1)}, u32[]{:S(2)}, u32[]{:S(2)}) collective-permute-start(bf16[384,64]{1,0:T(8,128)(2,1)S(1)} %shard_map.101.refs_12_), channel_id=1, source_target_pairs={{0,1},{1,0},{2,3},{3,2},{4,5},{5,4},{6,7},{7,6},{8,9},{9,8},{10,11... | collective-permute-start | bytes 147464 | tf_op jit(solution)/shard_map/ppermute | solution.py:383
  196.7 18.4 %copy-start.15 = (bf16[768,64]{1,0:T(8,128)(2,1)}, bf16[768,64]{1,0:T(8,128)(2,1)S(1)}, u32[]{:S(2)}) copy-start(bf16[768,64]{1,0:T(8,128)(2,1)S(1)} %pad_maximum_fusion.refs_11_) | copy-start | bytes 294916
  196.7 10.1 %collective-permute-start.24 = (bf16[768,64]{1,0:T(8,128)(2,1)S(1)}, bf16[768,64]{1,0:T(8,128)(2,1)S(1)}, u32[]{:S(2)}, u32[]{:S(2)}) collective-permute-start(bf16[768,64]{1,0:T(8,128)(2,1)S(1)} %pad_maximum_fusion.refs_11_), channel_id=1, source_target_pairs={{0,4},{1,5},{2,6},{3,7},{4,0},{5,1},{6,2},{7,3},{8,12},{9,13},{10,... | collective-permute-start | bytes 294920 | tf_op jit(solution)/shard_map/ppermute | solution.py:383
  197.5 17.6 %collective-permute-start.25 = (bf16[768,64]{1,0:T(8,128)(2,1)S(1)}, bf16[768,64]{1,0:T(8,128)(2,1)S(1)}, u32[]{:S(2)}, u32[]{:S(2)}) collective-permute-start(bf16[768,64]{1,0:T(8,128)(2,1)S(1)} %pad_maximum_fusion.refs_11_), channel_id=1, source_target_pairs={{0,8},{1,9},{2,10},{3,11},{4,12},{5,13},{6,14},{7,15},{8,0},{9,1},... | collective-permute-start | bytes 294920 | tf_op jit(solution)/shard_map/ppermute | solution.py:383
  200.9 14.2 %collective-permute-start.26 = (bf16[768,64]{1,0:T(8,128)(2,1)S(1)}, bf16[768,64]{1,0:T(8,128)(2,1)S(1)}, u32[]{:S(2)}, u32[]{:S(2)}) collective-permute-start(bf16[768,64]{1,0:T(8,128)(2,1)S(1)} %pad_maximum_fusion.refs_11_), channel_id=1, source_target_pairs={{0,12},{1,13},{2,14},{3,15},{4,8},{5,9},{6,10},{7,11},{8,4},{9,5},... | collective-permute-start | bytes 294920 | tf_op jit(solution)/shard_map/ppermute | solution.py:383
  215.1 13.1 %copy-start.14 = (bf16[16,64,1792]{2,1,0:T(8,128)(2,1)S(1)}, bf16[16,64,1792]{2,1,0:T(8,128)(2,1)}, u32[]{:S(2)}) copy-start(bf16[16,64,1792]{2,1,0:T(8,128)(2,1)} %refs_6_.13) | copy-start | bytes 11010052
  215.1 13.1 %copy-start.28 = (s32[65]{0:T(128)S(1)}, s32[65]{0:T(128)}, u32[]{:S(2)}) copy-start(s32[65]{0:T(128)} %pad_add_fusion.1.refs_0_) | copy-start | bytes 784
  215.1 24.2 %copy-start.1 = (s32[16]{0:T(128)S(1)}, s32[16]{0:T(128)}, u32[]{:S(2)}) copy-start(s32[16]{0:T(128)} %param.15) | copy-start | bytes 196
  (18 other events, 28.9 us)
